TPU v7x, 32 devices: a whole 2x2x4 slice. The times are simulated.
32 devices in a mesh: dp: 8 (over y, x, core), seq: 4 (over z).
Axes of the slice: x: 2, y: 2, z: 4, core: 2. Of those that a mesh axis runs over, the one named last changes fastest.
Arguments:
- tokens: bfloat16 [8, 1024, 1024], P('dp', 'seq'), may hold values from -6 to 6
- first_values: bfloat16 [8, 1024, 1024], P('dp', 'seq'), may hold values from -6 to 6
- out_grad: bfloat16 [8, 1024, 1024], P('dp', 'seq'), may hold values from -6 to 6
- segments: int32 [8, 1024], P('dp', 'seq'), may hold values from 0 to 3, as said below
- span_order: int32 [4], replicated, may hold values from 0 to 3, as said below
- qkv_weight: float32 [1024, 3072], P('dp'), may hold values from -0.1875 to 0.1875
- out_weight: float32 [1024, 1024], P('dp'), may hold values from -1 to 1
- gate_up_weight: float32 [1024, 5632], P('dp'), may hold values from -0.1875 to 0.1875
- down_weight: float32 [2816, 1024], P('dp'), may hold values from -0.109375 to 0.109375
- norm_gains: float32 [1024, 2], P('dp'), may hold values from 0.5 to 1.5
- first_qkv: float32 [1024, 3072], P('dp'), may hold values from -256 to 256
- first_out: float32 [1024, 1024], P('dp'), may hold values from -56 to 56
- first_gate_up: float32 [1024, 5632], P('dp'), may hold values from -192 to 192
- first_down: float32 [2816, 1024], P('dp'), may hold values from -256 to 256
- first_gains: float32 [1024, 2], P('dp'), may hold values from -512 to 512
- second_qkv: float32 [1024, 3072], P('dp'), may hold values from 2048 to 8192
- second_out: float32 [1024, 1024], P('dp'), may hold values from 81.92 to 327.68
- second_gate_up: float32 [1024, 5632], P('dp'), may hold values from 1003.52 to 4014.08
- second_down: float32 [2816, 1024], P('dp'), may hold values from 2048 to 8192
- second_gains: float32 [1024, 2], P('dp'), may hold values from 8192 to 32768
Outputs:
- layer_out: bfloat16 [8, 1024, 1024], P('dp', 'seq')
- tokens_grad: float32 [8, 1024, 1024], P('dp', 'seq')
- values_grad: float32 [8, 1024, 1024], P('dp', 'seq')
- new_qkv: float32 [1024, 3072], P('dp')
- new_out: float32 [1024, 1024], P('dp')
- new_gate_up: float32 [1024, 5632], P('dp')
- new_down: float32 [2816, 1024], P('dp')
- new_gains: float32 [1024, 2], P('dp')
- next_first_qkv: float32 [1024, 3072], P('dp')
- next_first_out: float32 [1024, 1024], P('dp')
- next_first_gate_up: float32 [1024, 5632], P('dp')
- next_first_down: float32 [2816, 1024], P('dp')
- next_first_gains: float32 [1024, 2], P('dp')
- next_second_qkv: float32 [1024, 3072], P('dp')
- next_second_out: float32 [1024, 1024], P('dp')
- next_second_gate_up: float32 [1024, 5632], P('dp')
- next_second_down: float32 [2816, 1024], P('dp')
- next_second_gains: float32 [1024, 2], P('dp')
Inputs may be any that keep to these rules, and one draw needn't show every extreme that they name: `segments`: read in order of positions, a sequence's ids never fall; every sequence has ids 0 to 3, and id 2 begins within the first 256 positions and ends within the last 256. `span_order`: A permutation of the span numbers.
All inputs are finite; a program needn't handle non-finite values.
Results may differ from a plain program's by a relative error of at most 0.015.
The roundings to bfloat16 on the way count: a program that leaves them out, or rounds other values in their place, can miss the bound.
Values may be sent and summed in bfloat16 or wider, within the bound.
A program may use at most 320 MiB of HBM per device.

v0:
```python
import math

import jax
import jax.numpy as jnp
from jax import lax
from jax.sharding import PartitionSpec as P

HEAD_DIM = 64
STEP = 10


NORM_EPS = 1e-06
ADAM_EPS = 1e-08
BLEND_MIX = 0.5
BETA_FIRST = 0.5
BETA_SECOND = 0.5
MATRIX_RATE = 0.06
MATRIX_DECAY = 0.1
GAIN_RATE = 0.5
ROPE_BASE = 10000.0
MASK_FILL = -1e30


def rounded(matrix):
    return lax.optimization_barrier(matrix.astype(jnp.bfloat16)).astype(jnp.float32)


def normalize_parts(matrix):
    inverse = lax.rsqrt(jnp.mean(matrix * matrix, axis=-1, keepdims=True) + NORM_EPS)
    return (matrix * inverse, inverse)


def norm_backward(grad_rows, scaled, inverse, gain_column):
    pushed = grad_rows * gain_column
    return inverse * (pushed - scaled * jnp.mean(pushed * scaled, axis=-1, keepdims=True))


def rotary(positions):
    half_width = HEAD_DIM // 2
    frequency = jnp.exp(
        jnp.arange(half_width, dtype=jnp.float32) * (-math.log(ROPE_BASE) / half_width)
    )
    angles = positions.astype(jnp.float32)[:, None] * frequency[None, :]
    return (jnp.cos(angles)[:, None, :], jnp.sin(angles)[:, None, :])


def rotate(head_rows, cosine, sine_table):
    half_width = head_rows.shape[-1] // 2
    lower_half = head_rows[..., :half_width]
    upper_half = head_rows[..., half_width:]
    return jnp.concatenate(
        [
            lower_half * cosine - upper_half * sine_table,
            upper_half * cosine + lower_half * sine_table,
        ],
        axis=-1,
    )


def unrotate(head_rows, cosine, sine_table):
    half_width = head_rows.shape[-1] // 2
    lower_half = head_rows[..., :half_width]
    upper_half = head_rows[..., half_width:]
    return jnp.concatenate(
        [
            lower_half * cosine + upper_half * sine_table,
            upper_half * cosine - lower_half * sine_table,
        ],
        axis=-1,
    )


def apply_adamw(master, first_state, second_state, gradient, rate, decay):
    next_first = BETA_FIRST * first_state + (1.0 - BETA_FIRST) * gradient
    next_second = BETA_SECOND * second_state + (1.0 - BETA_SECOND) * gradient * gradient
    first_hat = next_first / (1.0 - BETA_FIRST**STEP)
    second_hat = next_second / (1.0 - BETA_SECOND**STEP)
    new_master = master - rate * (first_hat / (jnp.sqrt(second_hat) + ADAM_EPS) + decay * master)
    return (new_master, next_first, next_second)


def as_blocks(key_flat, value_flat, segment_flat, block_rows, heads_count):
    block_count = key_flat.shape[0] // block_rows
    return (
        key_flat.reshape(block_count, block_rows, heads_count, HEAD_DIM),
        value_flat.reshape(block_count, block_rows, heads_count, HEAD_DIM),
        segment_flat.astype(jnp.float32).reshape(block_count, block_rows),
    )


def on_device(
    tokens,
    first_values,
    out_grad,
    segments,
    span_order,
    qkv_weight,
    out_weight,
    gate_up_weight,
    down_weight,
    norm_gains,
    first_qkv,
    first_out,
    first_gate_up,
    first_down,
    first_gains,
    second_qkv,
    second_out,
    second_gate_up,
    second_down,
    second_gains,
):
    qkv_copy, out_copy, gate_up_copy, down_copy, gains_copy = (
        lax.all_gather(qkv_weight.astype(jnp.bfloat16), "dp", axis=0, tiled=True),
        lax.all_gather(out_weight.astype(jnp.bfloat16), "dp", axis=0, tiled=True),
        lax.all_gather(gate_up_weight.astype(jnp.bfloat16), "dp", axis=0, tiled=True),
        lax.all_gather(down_weight.astype(jnp.bfloat16), "dp", axis=0, tiled=True),
        lax.all_gather(norm_gains.astype(jnp.bfloat16), "dp", axis=0, tiled=True),
    )
    gains_full = gains_copy.astype(jnp.float32)
    model_width = qkv_copy.shape[0]
    hidden_width = down_copy.shape[0]
    heads_count = model_width // HEAD_DIM
    residual = tokens[0].astype(jnp.float32)
    rows_here = residual.shape[0]
    span_count = lax.axis_size("seq")
    length = rows_here * span_count
    row_index = jnp.arange(length, dtype=jnp.int32)
    owner_table = (row_index // rows_here)[:, None] == jnp.arange(span_count, dtype=jnp.int32)[
        None, :
    ]
    positions = (
        jnp.sum(jnp.where(owner_table, span_order[None, :], 0), axis=1) * rows_here
        + row_index % rows_here
    )
    my_positions = lax.dynamic_slice_in_dim(
        positions, lax.axis_index("seq") * rows_here, rows_here, 0
    )
    my_segments = segments[0].astype(jnp.float32)
    cosine, sine_table = rotary(my_positions)
    score_scale = HEAD_DIM ** (-0.5)
    block_rows = min(512, length)
    block_count = length // block_rows
    position_blocks = positions.reshape(block_count, block_rows)
    scaled_in, inverse_in = normalize_parts(residual)
    normed_in = (scaled_in * gains_full[:, 0]).astype(jnp.bfloat16)
    mixed_rows = jnp.dot(normed_in, qkv_copy, preferred_element_type=jnp.float32)
    queries = rotate(
        mixed_rows[:, :model_width].reshape(rows_here, heads_count, HEAD_DIM), cosine, sine_table
    ).astype(jnp.bfloat16)
    keys_here = rotate(
        mixed_rows[:, model_width : 2 * model_width].reshape(rows_here, heads_count, HEAD_DIM),
        cosine,
        sine_table,
    ).astype(jnp.bfloat16)
    blended = (
        BLEND_MIX * mixed_rows[:, 2 * model_width :]
        + (1.0 - BLEND_MIX) * first_values[0].astype(jnp.float32)
    ).astype(jnp.bfloat16)
    keys_flat = keys_here.reshape(rows_here, model_width)
    segments_low = segments[0].astype(jnp.bfloat16)
    all_keys, all_values, all_segments = (
        lax.all_gather(keys_flat, "seq", axis=0, tiled=True),
        lax.all_gather(blended, "seq", axis=0, tiled=True),
        lax.all_gather(segments_low, "seq", axis=0, tiled=True),
    )
    key_blocks, value_blocks, segment_blocks = as_blocks(
        all_keys, all_values, all_segments, block_rows, heads_count
    )

    def block_allowed(segment_block, position_block):
        return (my_segments[:, None] == segment_block[None, :]) & (
            position_block[None, :] <= my_positions[:, None]
        )

    def block_scores(key_block):
        return (
            jnp.einsum("qhd,khd->hqk", queries, key_block, preferred_element_type=jnp.float32)
            * score_scale
        )

    def stats_step(carried, inputs):
        key_block, segment_block, position_block = inputs
        allowed = block_allowed(segment_block, position_block)
        highest_run, total_run = carried
        masked = jnp.where(allowed[None], block_scores(key_block), MASK_FILL)
        new_high = jnp.maximum(highest_run, jnp.max(masked, axis=-1))
        added = jnp.sum(
            jnp.where(allowed[None], jnp.exp(masked - new_high[..., None]), 0.0), axis=-1
        )
        return ((new_high, total_run * jnp.exp(highest_run - new_high) + added), None)

    start_state = (
        jnp.full((heads_count, rows_here), MASK_FILL, jnp.float32),
        jnp.zeros((heads_count, rows_here), jnp.float32),
    )
    (highest_all, total_all), unused = lax.scan(
        stats_step, start_state, (key_blocks, segment_blocks, position_blocks)
    )
    log_total = highest_all + jnp.log(total_all)

    def output_step(carried, inputs):
        key_block, value_block, segment_block, position_block = inputs
        allowed = block_allowed(segment_block, position_block)
        weights = jnp.where(
            allowed[None], jnp.exp(block_scores(key_block) - log_total[..., None]), 0.0
        ).astype(jnp.bfloat16)
        return (
            carried
            + jnp.einsum("hqk,khd->qhd", weights, value_block, preferred_element_type=jnp.float32),
            None,
        )

    attended_heads, unused = lax.scan(
        output_step,
        jnp.zeros((rows_here, heads_count, HEAD_DIM), jnp.float32),
        (key_blocks, value_blocks, segment_blocks, position_blocks),
    )
    attended_raw = attended_heads.reshape(rows_here, model_width)
    attended = attended_raw.astype(jnp.bfloat16)
    hidden_mid = residual + jnp.dot(attended, out_copy, preferred_element_type=jnp.float32)
    scaled_mid, inverse_mid = normalize_parts(hidden_mid)
    normed_mid = (scaled_mid * gains_full[:, 1]).astype(jnp.bfloat16)
    gate_up = jnp.dot(normed_mid, gate_up_copy, preferred_element_type=jnp.float32)
    gate_part = gate_up[:, :hidden_width]
    upward = gate_up[:, hidden_width:]
    sigmoid_gate = jax.nn.sigmoid(gate_part)
    swish_gate = gate_part * sigmoid_gate
    activation = (swish_gate * upward).astype(jnp.bfloat16)
    layer_out = (
        hidden_mid + jnp.dot(activation, down_copy, preferred_element_type=jnp.float32)
    ).astype(jnp.bfloat16)
    back_rows = out_grad[0]
    down_total = jnp.einsum("tf,td->fd", activation, back_rows, preferred_element_type=jnp.float32)
    activation_grad = jnp.einsum(
        "td,fd->tf", back_rows, down_copy, preferred_element_type=jnp.float32
    )
    gate_up_grad = jnp.concatenate(
        [
            activation_grad * upward * sigmoid_gate * (1.0 + gate_part * (1.0 - sigmoid_gate)),
            activation_grad * swish_gate,
        ],
        axis=1,
    ).astype(jnp.bfloat16)
    gate_up_total = jnp.einsum(
        "td,tf->df", normed_mid, gate_up_grad, preferred_element_type=jnp.float32
    )
    normed_mid_grad = jnp.einsum(
        "tf,df->td", gate_up_grad, gate_up_copy, preferred_element_type=jnp.float32
    )
    gain_mid_grad = jnp.sum(normed_mid_grad * scaled_mid, axis=0)
    hidden_mid_grad = back_rows.astype(jnp.float32) + norm_backward(
        normed_mid_grad, scaled_mid, inverse_mid, gains_full[:, 1]
    )
    mid_grad_low = hidden_mid_grad.astype(jnp.bfloat16)
    out_total = jnp.einsum("td,te->de", attended, mid_grad_low, preferred_element_type=jnp.float32)
    attended_grad = jnp.einsum(
        "te,de->td", mid_grad_low, out_copy, preferred_element_type=jnp.float32
    ).astype(jnp.bfloat16)
    heads_grad = attended_grad.reshape(rows_here, heads_count, HEAD_DIM)
    delta_rows = jnp.transpose(jnp.sum(heads_grad.astype(jnp.float32) * attended_heads, axis=-1))

    def grad_step(carried, inputs):
        key_block, value_block, segment_block, position_block = inputs
        allowed = block_allowed(segment_block, position_block)
        query_grad = carried
        weights = jnp.where(
            allowed[None], jnp.exp(block_scores(key_block) - log_total[..., None]), 0.0
        )
        weights_low = weights.astype(jnp.bfloat16)
        weights_grad = jnp.einsum(
            "qhd,khd->hqk", heads_grad, value_block, preferred_element_type=jnp.float32
        )
        scores_grad = (weights * (weights_grad - delta_rows[..., None])).astype(jnp.bfloat16)
        query_grad = (
            query_grad
            + jnp.einsum("hqk,khd->qhd", scores_grad, key_block, preferred_element_type=jnp.float32)
            * score_scale
        )
        key_grad = (
            jnp.einsum("hqk,qhd->khd", scores_grad, queries, preferred_element_type=jnp.float32)
            * score_scale
        )
        value_grad = jnp.einsum(
            "hqk,qhd->khd", weights_low, heads_grad, preferred_element_type=jnp.float32
        )
        query_grad, key_grad, value_grad = (query_grad, key_grad, value_grad)
        return (query_grad, (key_grad, value_grad))

    query_grad_all, block_grads = lax.scan(
        grad_step,
        jnp.zeros((rows_here, heads_count, HEAD_DIM), jnp.float32),
        (key_blocks, value_blocks, segment_blocks, position_blocks),
    )
    key_terms = block_grads[0].reshape(length, model_width)
    value_terms = block_grads[1].reshape(length, model_width)
    keys_home, blended_home = (
        lax.psum_scatter(key_terms, "seq", scatter_dimension=0, tiled=True),
        lax.psum_scatter(value_terms, "seq", scatter_dimension=0, tiled=True),
    )
    keys_grad = rounded(keys_home).reshape(rows_here, heads_count, HEAD_DIM)
    blended_grad = rounded(blended_home)
    queries_grad = rounded(query_grad_all)
    values_grad = ((1.0 - BLEND_MIX) * blended_grad)[None]
    mixed_grad = jnp.concatenate(
        [
            unrotate(queries_grad, cosine, sine_table).reshape(rows_here, model_width),
            unrotate(keys_grad, cosine, sine_table).reshape(rows_here, model_width),
            BLEND_MIX * blended_grad,
        ],
        axis=1,
    ).astype(jnp.bfloat16)
    qkv_total = jnp.einsum("td,te->de", normed_in, mixed_grad, preferred_element_type=jnp.float32)
    normed_in_grad = jnp.einsum(
        "te,de->td", mixed_grad, qkv_copy, preferred_element_type=jnp.float32
    )
    gain_in_grad = jnp.sum(normed_in_grad * scaled_in, axis=0)
    tokens_grad = (
        hidden_mid_grad + norm_backward(normed_in_grad, scaled_in, inverse_in, gains_full[:, 0])
    )[None]
    gains_total = jnp.stack([gain_in_grad, gain_mid_grad], axis=1)
    masters = (qkv_weight, out_weight, gate_up_weight, down_weight, norm_gains)
    firsts = (first_qkv, first_out, first_gate_up, first_down, first_gains)
    seconds = (second_qkv, second_out, second_gate_up, second_down, second_gains)
    rate_list = (MATRIX_RATE, MATRIX_RATE, MATRIX_RATE, MATRIX_RATE, GAIN_RATE)
    decays = (MATRIX_DECAY, MATRIX_DECAY, MATRIX_DECAY, MATRIX_DECAY, 0.0)
    reduced = (
        lax.psum_scatter(qkv_total, "dp", scatter_dimension=0, tiled=True),
        lax.psum_scatter(out_total, "dp", scatter_dimension=0, tiled=True),
        lax.psum_scatter(gate_up_total, "dp", scatter_dimension=0, tiled=True),
        lax.psum_scatter(down_total, "dp", scatter_dimension=0, tiled=True),
        lax.psum_scatter(gains_total, "dp", scatter_dimension=0, tiled=True),
    )
    reduced = lax.psum((reduced[0], reduced[1], reduced[2], reduced[3], reduced[4]), "seq")
    updated = [
        apply_adamw(
            masters[member],
            firsts[member],
            seconds[member],
            reduced[member],
            rate_list[member],
            decays[member],
        )
        for member in range(5)
    ]
    return (
        layer_out[None],
        tokens_grad,
        values_grad,
        updated[0][0],
        updated[1][0],
        updated[2][0],
        updated[3][0],
        updated[4][0],
        updated[0][1],
        updated[1][1],
        updated[2][1],
        updated[3][1],
        updated[4][1],
        updated[0][2],
        updated[1][2],
        updated[2][2],
        updated[3][2],
        updated[4][2],
    )


def solution(mesh):
    return jax.shard_map(
        on_device,
        mesh=mesh,
        in_specs=(
            P("dp", "seq", None),
            P("dp", "seq", None),
            P("dp", "seq", None),
            P("dp", "seq"),
            P(),
            P("dp", None),
            P("dp", None),
            P("dp", None),
            P("dp", None),
            P("dp", None),
            P("dp", None),
            P("dp", None),
            P("dp", None),
            P("dp", None),
            P("dp", None),
            P("dp", None),
            P("dp", None),
            P("dp", None),
            P("dp", None),
            P("dp", None),
        ),
        out_specs=(
            P("dp", "seq", None),
            P("dp", "seq", None),
            P("dp", "seq", None),
            P("dp", None),
            P("dp", None),
            P("dp", None),
            P("dp", None),
            P("dp", None),
            P("dp", None),
            P("dp", None),
            P("dp", None),
            P("dp", None),
            P("dp", None),
            P("dp", None),
            P("dp", None),
            P("dp", None),
            P("dp", None),
            P("dp", None),
        ),
        check_vma=False,
    )
```

profile of v0, /device:TPU:0, one launch (start us, length us, event | category | flops | bytes accessed | tf_op | source)
XLA Modules:
  0.0 1303.2 jit_solution(467723643911248073)
XLA Ops:
  9.8 10.2 all_gather.24
  20.2 38.5 %all-gather.8.cloned.1.call-done = bf16[1024,3072]{1,0:T(8,128)(2,1)} async-done(((bf16[128,3072]{1,0:T(8,128)(2,1)}), bf16[1024,3072]{1,0:T(8,128)(2,1)}) %all-gather.8.cloned.1.call-update) | async-done | bytes 6291472 | tf_op jit(solution)/shard_map/all_gather | solution.py:114
  58.8 4.7 fusion.87
  77.3 11.2 all-gather
  88.6 22.2 %all-gather.10.cloned.1.call-done = bf16[1024,1024]{1,0:T(8,128)(2,1)} async-done(((bf16[256,1024]{1,0:T(8,128)(2,1)}), bf16[1024,1024]{1,0:T(8,128)(2,1)}) %all-gather.10.cloned.1.call-update) | async-done | bytes 2097168 | tf_op jit(solution)/shard_map/all_gather | solution.py:164
  110.8 6.4 reshape.384
  117.2 5.5 copy.98
  122.8 35.2 %all-gather.12.cloned.1.call-done = bf16[1024,1024]{0,1:T(8,128)(2,1)} async-done(((bf16[256,1024]{0,1:T(8,128)(2,1)}), bf16[1024,1024]{0,1:T(8,128)(2,1)}) %all-gather.12.cloned.1.call-update) | async-done | bytes 2097168 | tf_op jit(solution)/shard_map/all_gather | solution.py:163
  158.0 4.5 reshape.362
  164.5 18.9 %while.39 = (s32[]{:T(128)}, f32[16,256]{1,0:T(8,128)S(1)}, f32[16,256]{1,0:T(8,128)S(1)}, f32[256]{0:T(256)S(1)}, f32[2,512]{1,0:T(2,128)S(1)}, /*index=5*/s32[...) while((s32[]{:T(128)}, f32[16,256]{1,0:T(8,128)S(1)}, ...), condition=%wide.region_5.6_spmd.clone, body=%wide.region_2.5_spmd.clone.sunk | while | flops 285626368 | bytes 18970764 | solution.py:197
  164.7 4.7 fusion.156
  169.4 4.5 select_reduce_fusion.3
  174.2 4.7 fusion.156
  178.8 4.5 select_reduce_fusion.3
  183.4 10.4 while.40
  183.7 4.7 fusion.162
  188.6 5.0 fusion.162
  199.8 56.7 %all-gather.16.cloned.1.call-done = bf16[1024,5632]{1,0:T(8,128)(2,1)} async-done(((bf16[128,5632]{1,0:T(8,128)(2,1)}), bf16[1024,5632]{1,0:T(8,128)(2,1)}) %all-gather.16.cloned.1.call-update) | async-done | bytes 11534352 | tf_op jit(solution)/shard_map/all_gather | solution.py:116
  256.5 10.3 fusion.104
  266.7 35.4 %all-gather.18.cloned.1.call-done = bf16[2816,1024]{1,0:T(8,128)(2,1)} async-done(((bf16[352,1024]{1,0:T(8,128)(2,1)}), bf16[2816,1024]{1,0:T(8,128)(2,1)}) %all-gather.18.cloned.1.call-update) | async-done | bytes 5767184 | tf_op jit(solution)/shard_map/all_gather | solution.py:117
  302.1 8.3 multiply_convert_fusion.1
  312.0 6.3 multiply_reduce_fusion
  325.4 119.4 %while.41 = (s32[]{:T(128)}, f32[256,16,64]{0,2,1:T(8,128)}, f32[2,512,16,64]{1,0,3,2:T(2,128)}, f32[2,512,16,64]{1,3,2,0:T(8,128)}, bf16[2,512,16,64]{1,3,2,0:T...) while((s32[]{:T(128)}, f32[256,16,64]{0,2,1:T(8,128)}, ...), condition=%wide.region_12.13_spmd.clone, body=%wide.region_11.12_spmd.clone.sunk | while | flops 1364852736 | bytes 135723376 | solution.py:290
  340.6 37.9 %dynamic_update_slice.13 = f32[2,512,16,64]{1,0,3,2:T(2,128)} dynamic-update-slice(f32[2,512,16,64]{1,0,3,2:T(2,128)} %get-tuple-element.848, f32[1,512,16,64]{1,0,3,2:T(1,128)S(1)} %copy.129, s32[]{:T(128)S(6)} %copy.151, s32[]{:T(128)} %constant.132.clone.1..sunk.2, s32[]{:T(128)} %constant.132.clone.1..sunk.2, s32[]{:T(128)} %constant.132.clone.1..sunk.2) | dynamic-update-slice | bytes 4194308 | tf_op jit(solution)/shard_map/while/body/jit(dynamic_update_index_in_dim)/dynamic_update_slice | solution.py:290
  378.5 6.6 bitcast_dynamic-update-slice_fusion.2
  388.1 4.2 fusion.174
  392.4 4.4 fusion.175
  400.3 37.9 %dynamic_update_slice.13 = f32[2,512,16,64]{1,0,3,2:T(2,128)} dynamic-update-slice(f32[2,512,16,64]{1,0,3,2:T(2,128)} %get-tuple-element.848, f32[1,512,16,64]{1,0,3,2:T(1,128)S(1)} %copy.129, s32[]{:T(128)S(6)} %copy.151, s32[]{:T(128)} %constant.132.clone.1..sunk.2, s32[]{:T(128)} %constant.132.clone.1..sunk.2, s32[]{:T(128)} %constant.132.clone.1..sunk.2) | dynamic-update-slice | bytes 4194308 | tf_op jit(solution)/shard_map/while/body/jit(dynamic_update_index_in_dim)/dynamic_update_slice | solution.py:290
  438.2 6.6 bitcast_dynamic-update-slice_fusion.2
  444.8 8.1 copy.112
  452.9 7.7 reshape.381
  460.6 5.1 copy.127
  471.4 7.3 fusion.79
  480.1 57.4 %reduce-scatter.12.cloned.1.call-done = f32[256,1024]{1,0:T(8,128)} async-done(((f32[1024,1024]{1,0:T(8,128)}), f32[256,1024]{1,0:T(8,128)}) %reduce-scatter.12.cloned.1.call-update) | async-done | bytes 1048592 | tf_op jit(solution)/shard_map/reduce_scatter | solution.py:299
  539.6 77.6 %reduce-scatter.10.cloned.1.call-done = f32[256,1024]{0,1:T(8,128)} async-done(((f32[1024,1024]{0,1:T(8,128)}), f32[256,1024]{0,1:T(8,128)}) %reduce-scatter.10.cloned.1.call-update) | async-done | bytes 1048592 | tf_op jit(solution)/shard_map/reduce_scatter | solution.py:298
  621.8 6.8 fusion.76
  630.0 11.5 fusion.54
  641.6 6.7 fusion.70
  649.4 23.0 %reduce-scatter.16.cloned.1.call-done = f32[128,1024]{1,0:T(8,128)} async-done(((f32[1024,1024]{1,0:T(8,128)}), f32[128,1024]{1,0:T(8,128)}) %reduce-scatter.16.cloned.1.call-update) | async-done | bytes 524304 | tf_op jit(solution)/shard_map/reduce_scatter | solution.py:329
  672.4 90.6 %reduce-scatter.20.cloned.1.call-done = f32[352,1024]{1,0:T(8,128)} async-done(((f32[2816,1024]{1,0:T(8,128)}), f32[352,1024]{1,0:T(8,128)}) %reduce-scatter.20.cloned.1.call-update) | async-done | bytes 1441808 | tf_op jit(solution)/shard_map/reduce_scatter | solution.py:331
  763.0 96.3 %reduce-scatter.14.cloned.1.call-done = f32[128,3072]{1,0:T(8,128)} async-done(((f32[1024,3072]{1,0:T(8,128)}), f32[128,3072]{1,0:T(8,128)}) %reduce-scatter.14.cloned.1.call-update) | async-done | bytes 1572880 | tf_op jit(solution)/shard_map/reduce_scatter | solution.py:328
  859.3 149.9 %reduce-scatter.18.cloned.1.call-done = f32[128,5632]{1,0:T(8,128)} async-done(((f32[1024,5632]{1,0:T(8,128)}), f32[128,5632]{1,0:T(8,128)}) %reduce-scatter.18.cloned.1.call-update) | async-done | bytes 2883600 | tf_op jit(solution)/shard_map/reduce_scatter | solution.py:330
  1009.2 5.6 fusion.63
  1016.1 31.2 %reduce-scatter.22.cloned.1.call-done = f32[128,2]{1,0:T(8,128)} async-done(((f32[1024,2]{1,0:T(8,128)}), f32[128,2]{1,0:T(8,128)}) %reduce-scatter.22.cloned.1.call-update) | async-done | bytes 1040
  1048.2 12.1 psum.39
  1060.9 217.1 %all-reduce.3.cloned.1.call-done = (f32[128,3072]{1,0:T(8,128)}, f32[128,1024]{1,0:T(8,128)}, f32[128,5632]{1,0:T(8,128)}, f32[352,1024]{1,0:T(8,128)}) async-done(((f32[128,3072]{1,0:T(8,128)}, f32[128,1024]{1,0:T(8,128)}, f32[128,5632]{1,0:T(8,128)}, f32[352,1024]{1,0:T(8,128)}), (f32[128,3072]{1,0:T(8,128)}, f32[128,1024]{1,0:T(8,128)}, f32[128,5632]{1,0:T(8,128)}, ...) | async-done | bytes 6422544 | tf_op jit(solution)/shard_map/psum | solution.py:334
  1278.0 6.0 multiply_subtract_fusion.1
  1287.2 5.1 multiply_subtract_fusion
  (233 shorter events, 81.5 us)
Async XLA Ops:
  7.2 12.8 copy-start.12
  7.2 51.5 %all-gather.8.cloned.1.call-start = ((), (), s32[]{:S(2)}) async-start(), calls=%async_computation.7 | async-start | bytes 7077888 | tf_op jit(solution)/shard_map/all_gather | solution.py:114
  9.7 101.1 %all-gather.10.cloned.1.call-start = ((), (), s32[]{:S(2)}) async-start(), calls=%async_computation.8 | async-start | bytes 2621440 | tf_op jit(solution)/shard_map/all_gather | solution.py:164
  20.2 43.3 %copy-start.42 = (f32[256]{0:T(256)}, f32[256]{0:T(256)S(1)}, u32[]{:S(2)}) copy-start(f32[256]{0:T(256)S(1)} %add_rsqrt_fusion.1) | copy-start | bytes 3076
  20.2 43.3 %copy-start.36 = (f32[1024,1]{0,1:T(1,128)}, f32[1024,1]{0,1:T(1,128)S(1)}, u32[]{:S(2)}) copy-start(f32[1024,1]{0,1:T(1,128)S(1)} %get-tuple-element.543) | copy-start | bytes 12292
  64.7 93.2 %all-gather.12.cloned.1.call-start = ((), (), s32[]{:S(2)}) async-start(), calls=%async_computation.9 | async-start | bytes 2621440 | tf_op jit(solution)/shard_map/all_gather | solution.py:163
  65.2 5.4 copy-start.38
  65.2 5.4 copy-start.40
  67.8 5.6 copy-start.9
  71.5 124.5 %all-gather.14.cloned.1.call-start = ((), (), s32[]{:S(2)}) async-start(), calls=%async_computation.10 | async-start | bytes 2359296 | tf_op jit(solution)/shard_map/all_gather | solution.py:115
  73.4 183.1 %all-gather.16.cloned.1.call-start = ((), (), s32[]{:S(2)}) async-start(), calls=%async_computation.11 | async-start | bytes 12976128 | tf_op jit(solution)/shard_map/all_gather | solution.py:116
  74.7 13.9 %copy-start.29 = (bf16[256,16,32]{0,2,1:T(8,128)(2,1)S(1)}, bf16[256,16,32]{0,2,1:T(8,128)(2,1)}, u32[]{:S(2)}) copy-start(bf16[256,16,32]{0,2,1:T(8,128)(2,1)} %get-tuple-element.532) | copy-start | bytes 786436
  74.7 13.9 %copy-start.30 = (bf16[256,16,32]{0,2,1:T(8,128)(2,1)S(1)}, bf16[256,16,32]{0,2,1:T(8,128)(2,1)}, u32[]{:S(2)}) copy-start(bf16[256,16,32]{0,2,1:T(8,128)(2,1)} %get-tuple-element.533) | copy-start | bytes 786436
  74.7 227.4 %all-gather.18.cloned.1.call-start = ((), (), s32[]{:S(2)}) async-start(), calls=%async_computation.12 | async-start | bytes 6488064 | tf_op jit(solution)/shard_map/all_gather | solution.py:117
  77.1 460.3 %reduce-scatter.12.cloned.1.call-start = ((), (), s32[]{:S(2)}) async-start(), calls=%async_computation.14 | async-start | bytes 5242880 | tf_op jit(solution)/shard_map/reduce_scatter | solution.py:299
  302.1 9.9 copy-start.5
  312.0 6.3 copy-start.22
  325.9 7.1 copy-start.2
  327.2 5.8 copy-start.1
  378.5 6.7 copy-start.3
  385.2 7.2 copy-start.2
  386.5 5.9 copy-start.1
  438.2 6.6 copy-start.3
  460.6 156.6 %reduce-scatter.10.cloned.1.call-start = ((), (), s32[]{:S(2)}) async-start(), calls=%async_computation.13 | async-start | bytes 5242880 | tf_op jit(solution)/shard_map/reduce_scatter | solution.py:298
  465.8 206.6 %reduce-scatter.16.cloned.1.call-start = ((), (), s32[]{:S(2)}) async-start(), calls=%async_computation.16 | async-start | bytes 4718592 | tf_op jit(solution)/shard_map/reduce_scatter | solution.py:329
  470.4 292.6 %reduce-scatter.20.cloned.1.call-start = ((), (), s32[]{:S(2)}) async-start(), calls=%async_computation.18 | async-start | bytes 12976128 | tf_op jit(solution)/shard_map/reduce_scatter | solution.py:331
  478.7 380.6 %reduce-scatter.14.cloned.1.call-start = ((), (), s32[]{:S(2)}) async-start(), calls=%async_computation.15 | async-start | bytes 14155776 | tf_op jit(solution)/shard_map/reduce_scatter | solution.py:328
  480.0 138.6 %copy-start.39 = (f32[256,32]{0,1:T(8,128)S(1)}, f32[256,32]{0,1:T(8,128)}, u32[]{:S(2)}) copy-start(f32[256,32]{0,1:T(8,128)} %copy-done.38) | copy-start | bytes 98308
  480.0 138.6 %copy-start.41 = (f32[256,32]{0,1:T(8,128)S(1)}, f32[256,32]{0,1:T(8,128)}, u32[]{:S(2)}) copy-start(f32[256,32]{0,1:T(8,128)} %copy-done.40) | copy-start | bytes 98308
  619.5 9.2 copy-start.21
  621.8 6.8 copy-start.24
  628.6 380.5 %reduce-scatter.18.cloned.1.call-start = ((), (), s32[]{:S(2)}) async-start(), calls=%async_computation.17 | async-start | bytes 25952256 | tf_op jit(solution)/shard_map/reduce_scatter | solution.py:330
  641.5 405.7 %reduce-scatter.22.cloned.1.call-start = ((), (), s32[]{:S(2)}) async-start(), calls=%async_computation.19 | async-start | bytes 589824
  649.4 628.6 %all-reduce.3.cloned.1.call-start = ((), (), s32[]{:S(2)}) async-start(), calls=%async_computation.20 | async-start | bytes 12845056 | tf_op jit(solution)/shard_map/psum | solution.py:334
  1009.2 5.6 copy-start.31
  1014.8 45.5 %copy-start.46 = (f32[128,2]{0,1:T(2,128)S(1)}, f32[128,2]{0,1:T(2,128)}, u32[]{:S(2)}) copy-start(f32[128,2]{0,1:T(2,128)} %param.35) | copy-start | bytes 3076
  1014.8 45.5 %copy-start.47 = (f32[128,2]{0,1:T(2,128)S(1)}, f32[128,2]{0,1:T(2,128)}, u32[]{:S(2)}) copy-start(f32[128,2]{0,1:T(2,128)} %param.40) | copy-start | bytes 3076
  1014.8 45.5 %copy-start.48 = (f32[128,2]{0,1:T(2,128)S(1)}, f32[128,2]{0,1:T(2,128)}, u32[]{:S(2)}) copy-start(f32[128,2]{0,1:T(2,128)} %param.45) | copy-start | bytes 3076
  1277.9 6.1 copy-start.19
  1277.9 6.1 copy-start.33
  1277.9 6.1 copy-start.34
  1277.9 6.1 copy-start.35
  1277.9 7.6 copy-start.15
  1278.0 7.6 copy-start.16
  1278.0 8.3 copy-start.17
  1287.2 5.1 copy-start.13
  1287.2 5.1 copy-start.25
  1287.2 5.1 copy-start.26
  (22 other events, 52.0 us)
Sparse Core Ops, SparseCore 0:
  10.5 48.2 all-gather.7
  64.8 45.9 all-gather.9
  113.0 44.9 all-gather.11
  160.3 26.1 all-gather.13
  188.7 67.6 all-gather.15
  258.8 43.3 all-gather.17
  460.7 76.7 reduce-scatter.11
  539.9 77.2 reduce-scatter.9
  620.6 51.8 reduce-scatter.15
  676.2 86.7 reduce-scatter.19
  766.9 92.3 reduce-scatter.13
  863.2 145.9 reduce-scatter.17
  1013.1 34.1 reduce-scatter.21
  1049.8 228.1 all-reduce.2
where the time goes:
time: 1310 us; the launch traced here: 1300 us
  waiting for transfers between devices  931 us (71%)
  local copies, waits for them, and re-layouts  139 us (11%)
  matrix products  130 us (10%)
  other arithmetic  52.5 us (4%)
  blocking collectives  33.5 us (3%)
  between operations  14.7 us (1%)
    psum x1, waiting for transfers between devices, on_device(): lax.psum((reduced[0], reduced[1], reduced[2], reduced[3], reduced[4]), 's...  217 us
    reduce_scatter x1, waiting for transfers between devices, on_device(): lax.psum_scatter(gate_up_total, 'dp', scatter_dimension=0, tiled=True)  150 us
    reduce_scatter x1, waiting for transfers between devices, on_device(): lax.psum_scatter(qkv_total, 'dp', scatter_dimension=0, tiled=True)  96.3 us
    reduce_scatter x1, waiting for transfers between devices, on_device(): lax.psum_scatter(down_total, 'dp', scatter_dimension=0, tiled=True)  90.6 us
    dynamic_update_slice x4, local copies, waits for them, and re-layouts, on_device(): lax.scan(grad_step, jnp.zeros((rows_here, heads_count, HEAD_DIM), jnp.flo...  80.1 us
    reduce_scatter x1, waiting for transfers between devices, on_device(): lax.psum_scatter(key_terms, 'seq', scatter_dimension=0, tiled=True)  77.6 us
    reduce_scatter x1, waiting for transfers between devices, on_device(): lax.psum_scatter(value_terms, 'seq', scatter_dimension=0, tiled=True)  57.4 us
    all_gather x1, waiting for transfers between devices, on_device(): lax.all_gather(gate_up_weight.astype(jnp.bfloat16), 'dp', axis=0, tiled=T...  56.7 us
  transfers between devices with their start and end apart: 14, of which 13 were waited for; matrix products, arithmetic and copies ran while one was open for 10% of the time, Pallas kernels for 0%

commit v1 on v0

v1 whole, which is shorter than its diff:
```python
import math

import jax
import jax.numpy as jnp
from jax import lax
from jax.sharding import PartitionSpec as P

HEAD_DIM = 64
STEP = 10


NORM_EPS = 1e-06
ADAM_EPS = 1e-08
BLEND_MIX = 0.5
BETA_FIRST = 0.5
BETA_SECOND = 0.5
MATRIX_RATE = 0.06
MATRIX_DECAY = 0.1
GAIN_RATE = 0.5
ROPE_BASE = 10000.0
MASK_FILL = -1e30
SCALE = HEAD_DIM ** (-0.5)

BF = jnp.bfloat16
F32 = jnp.float32


def dot_nn(left, right):
    return lax.dot_general(left, right, (((1,), (0,)), ((), ())), preferred_element_type=F32)


def dot_nt(left, right):
    return lax.dot_general(left, right, (((1,), (1,)), ((), ())), preferred_element_type=F32)


def dot_tn(left, right):
    return lax.dot_general(left, right, (((0,), (0,)), ((), ())), preferred_element_type=F32)


def normalize_parts(matrix):
    inverse = lax.rsqrt(jnp.mean(matrix * matrix, axis=-1, keepdims=True) + NORM_EPS)
    return (matrix * inverse, inverse)


def norm_backward(grad_rows, scaled, inverse, gain_column):
    pushed = grad_rows * gain_column
    return inverse * (pushed - scaled * jnp.mean(pushed * scaled, axis=-1, keepdims=True))


def rotary(positions):
    half_width = HEAD_DIM // 2
    frequency = jnp.exp(
        jnp.arange(half_width, dtype=F32) * (-math.log(ROPE_BASE) / half_width)
    )
    angles = positions.astype(F32)[:, None] * frequency[None, :]
    return (jnp.cos(angles)[:, None, :], jnp.sin(angles)[:, None, :])


def rotate(head_rows, cosine, sine_table):
    half_width = head_rows.shape[-1] // 2
    lower_half = head_rows[..., :half_width]
    upper_half = head_rows[..., half_width:]
    return jnp.concatenate(
        [
            lower_half * cosine - upper_half * sine_table,
            upper_half * cosine + lower_half * sine_table,
        ],
        axis=-1,
    )


def apply_adamw(master, first_state, second_state, gradient, rate, decay):
    next_first = BETA_FIRST * first_state + (1.0 - BETA_FIRST) * gradient
    next_second = BETA_SECOND * second_state + (1.0 - BETA_SECOND) * gradient * gradient
    first_hat = next_first / (1.0 - BETA_FIRST**STEP)
    second_hat = next_second / (1.0 - BETA_SECOND**STEP)
    new_master = master - rate * (first_hat / (jnp.sqrt(second_hat) + ADAM_EPS) + decay * master)
    return (new_master, next_first, next_second)


def to_heads(rows, span_count):
    return lax.all_to_all(
        rows.reshape(rows.shape[0], span_count, rows.shape[1] // span_count),
        "seq",
        split_axis=1,
        concat_axis=0,
        tiled=True,
    ).reshape(rows.shape[0] * span_count, rows.shape[1] // span_count)


def to_spans(columns, span_count):
    rows_here = columns.shape[0] // span_count
    got = lax.all_to_all(
        columns.reshape(span_count, rows_here, columns.shape[1]),
        "seq",
        split_axis=0,
        concat_axis=0,
        tiled=True,
    )
    return jnp.transpose(got, (1, 0, 2)).reshape(rows_here, columns.shape[1] * span_count)


def on_device(
    tokens,
    first_values,
    out_grad,
    segments,
    span_order,
    qkv_weight,
    out_weight,
    gate_up_weight,
    down_weight,
    norm_gains,
    first_qkv,
    first_out,
    first_gate_up,
    first_down,
    first_gains,
    second_qkv,
    second_out,
    second_gate_up,
    second_down,
    second_gains,
):
    span_count = lax.axis_size("seq")
    mine = lax.axis_index("seq")
    owned_rows, triple = qkv_weight.shape
    model_width = triple // 3
    group = model_width // span_count
    group_heads = group // HEAD_DIM
    residual = tokens[0].astype(F32)
    rows_here = residual.shape[0]
    length = rows_here * span_count
    hidden_width = gate_up_weight.shape[1] // 2

    qkv_owned = qkv_weight.reshape(owned_rows, 3, model_width).astype(BF)
    qkv_mine = lax.dynamic_slice_in_dim(qkv_owned, mine * group, group, 2).reshape(
        owned_rows, 3 * group
    )
    gains_owned = norm_gains.astype(BF).astype(F32)
    gains_full = lax.all_gather(norm_gains.astype(BF), "dp", axis=0, tiled=True).astype(F32)
    qkv_copy = lax.all_gather(qkv_mine, "dp", axis=0, tiled=True)
    out_copy = lax.all_gather(out_weight.astype(BF), "dp", axis=0, tiled=True)
    gate_up_copy = lax.all_gather(gate_up_weight.astype(BF), "dp", axis=0, tiled=True)
    down_copy = lax.all_gather(down_weight.astype(BF), "dp", axis=0, tiled=True)

    row_index = jnp.arange(length, dtype=jnp.int32)
    owner_table = (row_index // rows_here)[:, None] == jnp.arange(span_count, dtype=jnp.int32)[
        None, :
    ]
    positions = (
        jnp.sum(jnp.where(owner_table, span_order[None, :], 0), axis=1) * rows_here
        + row_index % rows_here
    )
    all_segments = lax.all_gather(segments[0], "seq", axis=0, tiled=True)
    cosine, sine_table = rotary(positions)
    allowed = (all_segments[:, None] == all_segments[None, :]) & (
        positions[None, :] <= positions[:, None]
    )

    scaled_in, inverse_in = normalize_parts(residual)
    normed_in = (scaled_in * gains_full[:, 0]).astype(BF)
    normed_all = lax.all_gather(normed_in, "seq", axis=0, tiled=True)
    first_all = to_heads(first_values[0], span_count)
    mixed = dot_nn(normed_all, qkv_copy)
    queries = rotate(
        mixed[:, :group].reshape(length, group_heads, HEAD_DIM), cosine, sine_table
    ).astype(BF)
    keys = rotate(
        mixed[:, group : 2 * group].reshape(length, group_heads, HEAD_DIM), cosine, sine_table
    ).astype(BF)
    blended = (
        (BLEND_MIX * mixed[:, 2 * group :] + (1.0 - BLEND_MIX) * first_all.astype(F32))
        .astype(BF)
        .reshape(length, group_heads, HEAD_DIM)
    )
    scores = jnp.einsum("qhd,khd->hqk", queries, keys, preferred_element_type=F32) * SCALE
    masked = jnp.where(allowed[None], scores, MASK_FILL)
    highest = jnp.max(masked, axis=-1, keepdims=True)
    raised = jnp.where(allowed[None], jnp.exp(masked - highest), 0.0)
    weights = raised / jnp.sum(raised, axis=-1, keepdims=True)
    weights_low = weights.astype(BF)
    attended_raw = jnp.einsum("hqk,khd->qhd", weights_low, blended, preferred_element_type=F32)
    attended = to_spans(attended_raw.reshape(length, group).astype(BF), span_count)

    hidden_mid = residual + dot_nn(attended, out_copy)
    scaled_mid, inverse_mid = normalize_parts(hidden_mid)
    normed_mid = (scaled_mid * gains_full[:, 1]).astype(BF)
    gate_up = dot_nn(normed_mid, gate_up_copy)
    gate_part = gate_up[:, :hidden_width]
    upward = gate_up[:, hidden_width:]
    sigmoid_gate = jax.nn.sigmoid(gate_part)
    swish_gate = gate_part * sigmoid_gate
    activation = (swish_gate * upward).astype(BF)
    layer_out = (hidden_mid + dot_nn(activation, down_copy)).astype(BF)
    back_rows = out_grad[0]
    activation_grad = dot_nt(back_rows, down_copy)
    gate_up_grad = jnp.concatenate(
        [
            activation_grad * upward * sigmoid_gate * (1.0 + gate_part * (1.0 - sigmoid_gate)),
            activation_grad * swish_gate,
        ],
        axis=1,
    ).astype(BF)
    normed_mid_grad = dot_nt(gate_up_grad, gate_up_copy)
    hidden_mid_grad = back_rows.astype(F32) + norm_backward(
        normed_mid_grad, scaled_mid, inverse_mid, gains_full[:, 1]
    )
    mid_grad_low = hidden_mid_grad.astype(BF)
    attended_grad = to_heads(dot_nt(mid_grad_low, out_copy).astype(BF), span_count)

    heads_grad = attended_grad.reshape(length, group_heads, HEAD_DIM)
    delta = jnp.transpose(jnp.sum(heads_grad.astype(F32) * attended_raw, axis=-1))
    weights_grad = jnp.einsum("qhd,khd->hqk", heads_grad, blended, preferred_element_type=F32)
    scores_grad = (weights * (weights_grad - delta[..., None])).astype(BF)
    queries_grad = (
        jnp.einsum("hqk,khd->qhd", scores_grad, keys, preferred_element_type=F32) * SCALE
    ).astype(BF).astype(F32)
    keys_grad = (
        jnp.einsum("hqk,qhd->khd", scores_grad, queries, preferred_element_type=F32) * SCALE
    ).astype(BF).astype(F32)
    blended_grad = jnp.einsum(
        "hqk,qhd->khd", weights_low, heads_grad, preferred_element_type=F32
    ).astype(BF).reshape(length, group)
    values_grad = (1.0 - BLEND_MIX) * to_spans(blended_grad, span_count).astype(F32)
    mixed_grad = jnp.concatenate(
        [
            rotate(queries_grad, cosine, -sine_table).reshape(length, group),
            rotate(keys_grad, cosine, -sine_table).reshape(length, group),
            BLEND_MIX * blended_grad.astype(F32),
        ],
        axis=1,
    ).astype(BF)
    normed_in_grad = lax.psum_scatter(
        dot_nt(mixed_grad, qkv_copy).astype(BF), "seq", scatter_dimension=0, tiled=True
    ).astype(F32)
    tokens_grad = hidden_mid_grad + norm_backward(
        normed_in_grad, scaled_in, inverse_in, gains_full[:, 0]
    )

    def to_owner(terms):
        return lax.psum_scatter(terms.astype(BF), "dp", scatter_dimension=0, tiled=True)

    qkv_part = lax.all_gather(to_owner(dot_tn(normed_all, mixed_grad)), "seq", axis=0)
    qkv_total = (
        jnp.transpose(qkv_part.reshape(span_count, owned_rows, 3, group), (1, 2, 0, 3))
        .reshape(owned_rows, triple)
        .astype(F32)
    )
    out_total, gate_up_total, down_total = lax.psum(
        (
            to_owner(dot_tn(attended, mid_grad_low)),
            to_owner(dot_tn(normed_mid, gate_up_grad)),
            to_owner(dot_tn(activation, back_rows)),
        ),
        "seq",
    )
    out_total, gate_up_total, down_total = (
        out_total.astype(F32),
        gate_up_total.astype(F32),
        down_total.astype(F32),
    )
    gains_total = jnp.stack(
        [
            jnp.sum(qkv_total * qkv_weight.astype(BF).astype(F32), axis=1),
            jnp.sum(gate_up_total * gate_up_weight.astype(BF).astype(F32), axis=1),
        ],
        axis=1,
    ) / gains_owned
    masters = (qkv_weight, out_weight, gate_up_weight, down_weight, norm_gains)
    firsts = (first_qkv, first_out, first_gate_up, first_down, first_gains)
    seconds = (second_qkv, second_out, second_gate_up, second_down, second_gains)
    totals = (qkv_total, out_total, gate_up_total, down_total, gains_total)
    rate_list = (MATRIX_RATE, MATRIX_RATE, MATRIX_RATE, MATRIX_RATE, GAIN_RATE)
    decays = (MATRIX_DECAY, MATRIX_DECAY, MATRIX_DECAY, MATRIX_DECAY, 0.0)
    updated = [
        apply_adamw(masters[i], firsts[i], seconds[i], totals[i], rate_list[i], decays[i])
        for i in range(5)
    ]
    return (
        (layer_out[None], tokens_grad[None], values_grad[None])
        + tuple(member[0] for member in updated)
        + tuple(member[1] for member in updated)
        + tuple(member[2] for member in updated)
    )


def solution(mesh):
    rows = P("dp", "seq", None)
    owned = P("dp", None)
    return jax.shard_map(
        on_device,
        mesh=mesh,
        in_specs=(rows, rows, rows, P("dp", "seq"), P()) + (owned,) * 15,
        out_specs=(rows,) * 3 + (owned,) * 15,
        check_vma=False,
    )
```

time: 1310 us -> 674 us (0.51)
  waiting for transfers between devices: 931 us -> 380 us
  local copies, waits for them, and re-layouts: 139 us -> 42.2 us
  blocking collectives: 33.5 us -> 70.9 us
  matrix products: 130 us -> 97.7 us
    reduce_scatter x6 -> x5, waiting for transfers between devices: 495 us -> 149 us  [the longest x4 143 us: to_owner(): lax.psum_scatter(terms.astype(BF), 'dp', scatter_dimension=0, tiled=True)]
    psum x1, waiting for transfers between devices: 217 us -> 97.6 us  [on_device(): lax.psum((to_owner(dot_tn(attended, mid_grad_low)), to_owner(dot_tn(norme...]
    dynamic_update_slice x4 -> x0, local copies, waits for them, and re-layouts: 80.1 us -> none  [on_device(): lax.scan(grad_step, jnp.zeros((rows_here, heads_count, HEAD_DIM), jnp.flo...]
    all_gather x6 -> x5, waiting for transfers between devices: 188 us -> 119 us  [the longest x1 47.4 us: on_device(): lax.all_gather(gate_up_weight.astype(BF), 'dp', axis=0, tiled=True)]
    dot_general x26 -> x17, matrix products: 130 us -> 85.5 us  [the longest x4 24.4 us: dot_nt(): lax.dot_general(left, right, (((1,), (1,)), ((), ())), preferred_element_...]
    unnamed x15 -> x11, waiting for transfers between devices: 31.4 us -> 0.18 us
    all_gather x2 -> x3, blocking collectives: 21.4 us -> 51.2 us  [the longest x1 26 us: on_device(): lax.all_gather(to_owner(dot_tn(normed_all, mixed_grad)), 'seq', axis=0)]
    reshape x7 -> x1, local copies, waits for them, and re-layouts: 27.1 us -> 2.04 us  [to_heads(): rows.reshape(rows.shape[0], span_count, rows.shape[1] // span_count)]
  transfers between devices with their start and end apart: 14 -> 14, of which waited for: 13 -> 9; matrix products, arithmetic and copies ran while one was open for 10% -> 22% of each run, Pallas kernels for 0% -> 0%
where the time goes in v1:
time: 674 us; the launch traced here: 664 us
  waiting for transfers between devices  380 us (56%)
  matrix products  97.7 us (14%)
  blocking collectives  70.9 us (11%)
  other arithmetic  44.8 us (7%)
  local copies, waits for them, and re-layouts  42.2 us (6%)
  between operations  14.8 us (2%)
  starting transfers between devices  13.3 us (2%)
    reduce_scatter x4, waiting for transfers between devices, to_owner(): lax.psum_scatter(terms.astype(BF), 'dp', scatter_dimension=0, tiled=True)  143 us
    psum x1, waiting for transfers between devices, on_device(): lax.psum((to_owner(dot_tn(attended, mid_grad_low)), to_owner(dot_tn(norme...  97.6 us
    all_gather x1, waiting for transfers between devices, on_device(): lax.all_gather(gate_up_weight.astype(BF), 'dp', axis=0, tiled=True)  47.4 us
    all_gather x1, waiting for transfers between devices, on_device(): down_copy = lax.all_gather(down_weight.astype(BF), 'dp', axis=0, tiled=True)  36.2 us
    all_gather x1, waiting for transfers between devices, on_device(): normed_all = lax.all_gather(normed_in, 'seq', axis=0, tiled=True)  35.1 us
    all_gather x1, blocking collectives, on_device(): lax.all_gather(to_owner(dot_tn(normed_all, mixed_grad)), 'seq', axis=0)  26 us
    dot_general x4, matrix products, dot_nt(): lax.dot_general(left, right, (((1,), (1,)), ((), ())), preferred_element_...  24.4 us
    unnamed x81, local copies, waits for them, and re-layouts  23.2 us
  transfers between devices with their start and end apart: 14, of which 9 were waited for; matrix products, arithmetic and copies ran while one was open for 22% of the time, Pallas kernels for 0%

profile of v1, /device:TPU:0, one launch (start us, length us, event | category | flops | bytes accessed | tf_op | source)
XLA Modules:
  0.0 663.8 jit_solution(13883405167433386910)
XLA Ops:
  11.9 10.2 %all_gather.27 = bf16[1024,2]{0,1:T(2,128)(2,1)S(1)} all-gather(bf16[128,2]{0,1:T(2,128)(2,1)S(1)} %convert_element_type.185), channel_id=1, replica_groups=mesh['dp'=8,'seq'=4] {'dp'}, dimensions={0}, use_global_device_ids=true | all-gather | bytes 4608 | tf_op jit(solution)/shard_map/all_gather | solution.py:141
  24.2 3.2 convert_element_type.201
  29.5 4.9 all-to-all-start
  34.3 15.0 %all-gather = s32[1,1024]{1,0:T(1,128)S(1)} all-gather(s32[1,256]{1,0:T(1,128)S(1)} %copy-done.28), channel_id=2, replica_groups=mesh['dp'=8,'seq'=4] {'seq'}, dimensions={1}, use_global_device_ids=true | all-gather | bytes 5120 | tf_op jit(solution)/shard_map/all_gather | solution.py:155
  53.6 35.1 %all-gather.8.cloned.1.call-done = bf16[1024,1024]{1,0:T(8,128)(2,1)} async-done(((bf16[256,1024]{1,0:T(8,128)(2,1)}), bf16[1024,1024]{1,0:T(8,128)(2,1)}) %all-gather.8.cloned.1.call-update) | async-done | bytes 2097168 | tf_op jit(solution)/shard_map/all_gather | solution.py:163
  88.7 3.9 fusion.79
  95.0 12.3 %fusion.77 = (f32[4,1024]{1,0:T(4,128)S(1)}, f32[4,1024,1024]{1,2,0:T(8,128)}) fusion(pred[1024,1024]{0,1:T(8,128)(4,1)S(1)} %copy-done.19, bf16[1024,4,32]{0,2,1:T(8,128)(2,1)} %get-tuple-element.108, bf16[1024,4,32]{0,2,1:T(8,128)(2,1)} %get-tuple-element.109, bf16[1024,4,32]{0,2,1:T(8,128)(2,1)S(1)} %get-tuple-element.103, ...), kind=kOutput, calls=%fused_computation.147 | convolution fusion | flops 559940608 | bytes 18890752 | tf_op jit(solution)/shard_map/sub | solution.py:180
  107.2 7.4 %fusion.5 = bf16[4,1024,1024]{1,2,0:T(8,128)(2,1)S(1)} fusion(f32[4,1024,1024]{1,2,0:T(8,128)} %get-tuple-element.118, f32[4,1024]{1,0:T(4,128)S(1)} %get-tuple-element.117), kind=kLoop, calls=%fused_computation.10 | loop fusion | flops 8388608 | bytes 25182208 | tf_op jit(solution)/shard_map/convert_element_type | solution.py:182
  114.6 3.1 fusion.78
  119.5 3.5 all-to-all-start.1
  123.2 14.5 %all-to-all-done.1 = bf16[4,256,256]{1,2,0:T(8,128)(2,1)S(1)} async-done(((bf16[4,256,256]{1,2,0:T(8,128)(2,1)}), bf16[4,256,256]{1,2,0:T(8,128)(2,1)S(1)}, u32[]{:S(2)}, u32[]{:S(2)}) %all-to-all-start.1) | async-done | bytes 524320 | tf_op jit(solution)/shard_map/all_to_all | solution.py:93
  137.7 2.6 multiply_reduce_fusion.2
  140.3 47.4 %all-gather.14.cloned.1.call-done = bf16[1024,5632]{1,0:T(8,128)(2,1)} async-done(((bf16[128,5632]{1,0:T(8,128)(2,1)}), bf16[1024,5632]{1,0:T(8,128)(2,1)}) %all-gather.14.cloned.1.call-update) | async-done | bytes 11534352 | tf_op jit(solution)/shard_map/all_gather | solution.py:144
  187.8 9.4 %fusion.68 = f32[256,5632]{1,0:T(8,128)} fusion(bf16[1024,5632]{1,0:T(8,128)(2,1)} %all-gather.14.cloned.1.call-done, f32[256,1024]{1,0:T(8,128)S(1)} %get-tuple-element.122, f32[1024]{0:T(1024)S(1)} %bitcast.123, f32[256]{0:T(256)S(1)} %add_rsqrt_fusion), kind=kOutput, calls=%fused_computation.144 | convolution fusion | flops 2953576448 | bytes 18355200 | tf_op jit(solution)/shard_map/dot_general | solution.py:29
  197.2 36.2 %all-gather.16.cloned.1.call-done = bf16[2816,1024]{1,0:T(8,128)(2,1)} async-done(((bf16[352,1024]{1,0:T(8,128)(2,1)}), bf16[2816,1024]{1,0:T(8,128)(2,1)}) %all-gather.16.cloned.1.call-update) | async-done | bytes 5767184 | tf_op jit(solution)/shard_map/all_gather | solution.py:145
  233.4 8.9 %multiply_convert_fusion.2 = (bf16[256,2816]{1,0:T(8,128)(2,1)S(1)}, bf16[256,2816]{1,0:T(8,128)(2,1)S(1)}, bf16[256,2816]{1,0:T(8,128)(2,1)}) fusion(f32[256,5632]{1,0:T(8,128)} %fusion.68, bf16[2816,1024]{1,0:T(8,128)(2,1)} %all-gather.16.cloned.1.call-done, bf16[1,256,1024]{2,1,0:T(8,128)(2,1)S(1)} %copy-done.13), kind=kOutput, calls=%fused_computation.22 | convolution fusion | flops 1487208448 | bytes 16384000 | tf_op jit(solution)/shard_map/dot_general | solution.py:33
  242.3 7.3 %multiply_reduce_fusion.1 = (f32[256]{0:T(256)S(1)}, f32[256,1024]{1,0:T(8,128)S(1)}) fusion(f32[256,1024]{1,0:T(8,128)S(1)} %get-tuple-element.122, f32[256]{0:T(256)S(1)} %add_rsqrt_fusion, f32[1024]{0:T(1024)S(1)} %bitcast.124, bf16[1024,5632]{1,0:T(8,128)(2,1)} %all-gather.14.cloned.1.call-done, bf16[256,2816]{1,0:T(8,128)(2,1)S(1)} %get-tuple-element.91, ...), kind=kOutput, calls=%fused_computation.80 | convolution fusion | flops 2959605504 | bytes 16521216 | tf_op jit(solution)/shard_map/dot_general | solution.py:33
  252.8 5.7 convolution_convert_fusion.1
  258.6 8.1 %convolution_convert_fusion = bf16[1024,5632]{1,0:T(8,128)(2,1)} fusion(bf16[256,2816]{1,0:T(8,128)(2,1)} %copy-done.18, bf16[256,2816]{1,0:T(8,128)(2,1)} %copy-done.17, f32[256,1024]{1,0:T(8,128)S(1)} %get-tuple-element.122, f32[1024]{0:T(1024)S(1)} %bitcast.125, f32[256]{0:T(256)S(1)} %add_rsqrt_fusion), kind=kOutput, calls=%fused_computation.5 | convolution fusion | flops 2965110784 | bytes 15471616 | tf_op jit(solution)/shard_map/dot_general | solution.py:37
  266.8 3.2 convolution_convert_fusion.6
  272.0 19.7 %all_to_all.34 = bf16[256,4,256]{0,2,1:T(8,128)(2,1)S(1)} all-to-all(bf16[256,4,256]{0,2,1:T(8,128)(2,1)} %bitcast.111), channel_id=1, replica_groups=mesh['dp'=8,'seq'=4] {'seq'}, dimensions={1} | all-to-all | bytes 1048576 | tf_op jit(solution)/shard_map/all_to_all | solution.py:82
  292.9 2.2 reshape_reshape.6
  296.6 8.6 %multiply_convert_fusion = bf16[4,1024,1024]{1,2,0:T(8,128)(2,1)S(1)} fusion(bf16[1024,4,64]{0,2,1:T(8,128)(2,1)} %reshape_reshape.6, bf16[1024,4,64]{0,2,1:T(8,128)(2,1)} %bitcast.113, f32[4,1024]{1,0:T(4,128)S(1)} %bitcast.130, f32[4,1024,1024]{1,2,0:T(8,128)} %get-tuple-element.118, f32[4,1024]{1,0:T(4,128)S(1)} %get-tuple-element.117), kind=kOutput, calls=%fused_computation.1 | convolution fusion | flops 553648128 | bytes 26247168 | tf_op jit(solution)/shard_map/qhd,khd->hqk/dot_general | solution.py:214
  305.2 2.9 fusion.23
  308.1 2.7 fusion.26
  311.9 3.5 multiply_convert_fusion.4
  316.2 3.0 convolution_convert_fusion.4
  319.5 5.1 convolution_convert_fusion.3
  324.6 2.2 reshape_reshape.7
  328.8 4.1 all-to-all-start.3
  333.0 24.0 %reduce-scatter.14.cloned.1.call-done = bf16[352,1024]{1,0:T(8,128)(2,1)} async-done(((bf16[2816,1024]{1,0:T(8,128)(2,1)}), bf16[352,1024]{1,0:T(8,128)(2,1)}) %reduce-scatter.14.cloned.1.call-update) | async-done | bytes 720912 | tf_op jit(solution)/shard_map/reduce_scatter | solution.py:242
  357.0 90.3 %reduce-scatter.12.cloned.1.call-done = bf16[128,5632]{1,0:T(8,128)(2,1)} async-done(((bf16[1024,5632]{1,0:T(8,128)(2,1)}), bf16[128,5632]{1,0:T(8,128)(2,1)}) %reduce-scatter.12.cloned.1.call-update) | async-done | bytes 1441808 | tf_op jit(solution)/shard_map/reduce_scatter | solution.py:242
  447.4 3.0 copy.100
  450.4 3.0 copy.103
  453.4 5.6 fusion.28
  461.4 28.3 %reduce-scatter.8.cloned.1.call-done = bf16[128,768]{1,0:T(8,128)(2,1)} async-done(((bf16[1024,768]{1,0:T(8,128)(2,1)}), bf16[128,768]{1,0:T(8,128)(2,1)}) %reduce-scatter.8.cloned.1.call-update) | async-done | bytes 196624 | tf_op jit(solution)/shard_map/reduce_scatter | solution.py:242
  489.7 26.0 %all-gather.1 = bf16[512,768]{1,0:T(8,128)(2,1)S(1)} all-gather(bf16[128,768]{1,0:T(8,128)(2,1)} %reduce-scatter.8.cloned.1.call-done), channel_id=3, replica_groups=mesh['dp'=8,'seq'=4] {'seq'}, dimensions={0}, use_global_device_ids=true | all-gather | bytes 983040 | tf_op jit(solution)/shard_map/all_gather | solution.py:244
  517.1 2.7 reshape.322
  522.3 4.7 multiply_subtract_fusion.1
  527.0 3.0 copy.107
  530.0 3.0 copy.108
  533.0 3.0 copy.109
  536.1 6.4 reduce-scatter.6.cloned.1.call-done
  543.9 2.3 fusion.34
  546.2 97.6 %all-reduce.3.cloned.1.call-done = (bf16[128,1024]{1,0:T(8,128)(2,1)}, bf16[128,5632]{1,0:T(8,128)(2,1)}, bf16[352,1024]{1,0:T(8,128)(2,1)}) async-done(((bf16[128,1024]{1,0:T(8,128)(2,1)}, bf16[128,5632]{1,0:T(8,128)(2,1)}, bf16[352,1024]{1,0:T(8,128)(2,1)}), (bf16[128,1024]{1,0:T(8,128)(2,1)}, bf16[128,5632]{1,0:T(8,128)(2,1)}, bf16[352,1024]{1,0:T(8,128)(2,1)})) %all-reduce.3.cloned.1.call-update) | async-done | bytes 2424848 | tf_op jit(solution)/shard_map/psum | solution.py:250
  643.8 2.8 multiply_subtract_fusion.3
  646.6 6.7 %multiply_subtract_fusion = (f32[128,5632]{1,0:T(8,128)}, f32[128,5632]{1,0:T(8,128)}, f32[128,5632]{1,0:T(8,128)}, f32[128]{0:T(128)S(1)}) fusion(f32[128,5632]{1,0:T(8,128)S(1)} %copy-done.4, bf16[128,5632]{1,0:T(8,128)(2,1)} %get-tuple-element.73, f32[128,5632]{1,0:T(8,128)} %param.32, f32[128,5632]{1,0:T(8,128)} %param.37), kind=kLoop, calls=%fused_computation.20 | loop fusion | flops 13696896 | bytes 18743808 | tf_op jit(solution)/shard_map/sub | solution.py:77
  653.4 2.8 multiply_subtract_fusion.2
  (141 shorter events, 37.9 us)
Async XLA Ops:
  7.2 46.4 %all-gather.10.cloned.1.call-start = ((), (), s32[]{:S(2)}) async-start(), calls=%async_computation.10 | async-start | bytes 1769472 | tf_op jit(solution)/shard_map/all_gather | solution.py:142
  7.2 4.6 copy-start.29
  7.2 14.8 %copy-start.3 = (bf16[1,256,1024]{2,1,0:T(8,128)(2,1)S(1)}, bf16[1,256,1024]{2,1,0:T(8,128)(2,1)}, u32[]{:S(2)}) copy-start(bf16[1,256,1024]{2,1,0:T(8,128)(2,1)} %param.20) | copy-start | bytes 1572868
  9.2 14.9 %copy-start.1 = (f32[128,3072]{0,1:T(8,128)}, f32[128,3072]{0,1:T(8,128)S(1)}, u32[]{:S(2)}) copy-start(f32[128,3072]{0,1:T(8,128)S(1)} %copy.88) | copy-start | bytes 4718596
  9.2 14.2 %copy-start.11 = (f32[128,1024]{1,0:T(8,128)S(1)}, f32[128,1024]{1,0:T(8,128)}, u32[]{:S(2)}) copy-start(f32[128,1024]{1,0:T(8,128)} %param.26) | copy-start | bytes 1572868
  11.8 76.9 %all-gather.8.cloned.1.call-start = ((), (), s32[]{:S(2)}) async-start(), calls=%async_computation.9 | async-start | bytes 2621440 | tf_op jit(solution)/shard_map/all_gather | solution.py:163
  23.3 99.9 %all-gather.12.cloned.1.call-start = ((), (), s32[]{:S(2)}) async-start(), calls=%async_computation.11 | async-start | bytes 2359296 | tf_op jit(solution)/shard_map/all_gather | solution.py:143
  24.1 3.3 copy-start.6
  24.1 163.6 %all-gather.14.cloned.1.call-start = ((), (), s32[]{:S(2)}) async-start(), calls=%async_computation.12 | async-start | bytes 12976128 | tf_op jit(solution)/shard_map/all_gather | solution.py:144
  27.4 1.1 copy-start.24
  27.4 7.0 %copy-start.28 = (s32[1,256]{1,0:T(1,128)S(1)}, s32[1,256]{1,0:T(1,128)}, u32[]{:S(2)}) copy-start(s32[1,256]{1,0:T(1,128)} %param.23) | copy-start | bytes 3076
  27.4 22.0 %copy-start.32 = (s32[4]{0:T(128)S(1)}, s32[4]{0:T(128)}, u32[]{:S(2)}) copy-start(s32[4]{0:T(128)} %param.24) | copy-start | bytes 52
  27.4 206.0 %all-gather.16.cloned.1.call-start = ((), (), s32[]{:S(2)}) async-start(), calls=%async_computation.13 | async-start | bytes 6488064 | tf_op jit(solution)/shard_map/all_gather | solution.py:145
  29.5 23.1 %all-to-all-start = ((bf16[256,4,256]{0,2,1:T(8,128)(2,1)}), bf16[256,4,256]{0,2,1:T(8,128)(2,1)S(1)}, u32[]{:S(2)}, u32[]{:S(2)}) async-start(bf16[256,4,256]{0,2,1:T(8,128)(2,1)} %bitcast.5), calls=%async_computation | async-start | bytes 1048576 | tf_op jit(solution)/shard_map/all_to_all | solution.py:82
  93.8 1.2 copy-start.19
  94.9 12.4 %copy-start.20 = (bf16[1024,4,32]{0,2,1:T(8,128)(2,1)}, bf16[1024,4,32]{0,2,1:T(8,128)(2,1)S(1)}, u32[]{:S(2)}) copy-start(bf16[1024,4,32]{0,2,1:T(8,128)(2,1)S(1)} %get-tuple-element.103) | copy-start | bytes 786436
  107.2 7.4 %copy-start.12 = (bf16[1024,256]{0,1:T(8,128)(2,1)S(1)}, bf16[1024,256]{0,1:T(8,128)(2,1)}, u32[]{:S(2)}) copy-start(bf16[1024,256]{0,1:T(8,128)(2,1)} %get-tuple-element.95) | copy-start | bytes 1572868
  114.6 3.6 copy-start
  119.5 18.2 %all-to-all-start.1 = ((bf16[4,256,256]{1,2,0:T(8,128)(2,1)}), bf16[4,256,256]{1,2,0:T(8,128)(2,1)S(1)}, u32[]{:S(2)}, u32[]{:S(2)}) async-start(bf16[4,256,256]{1,2,0:T(8,128)(2,1)} %copy.92), calls=%async_computation.1 | async-start | bytes 1048576 | tf_op jit(solution)/shard_map/all_to_all | solution.py:93
  123.0 210.0 %reduce-scatter.10.cloned.1.call-start = ((), (), s32[]{:S(2)}) async-start(), calls=%async_computation.16 | async-start | bytes 2359296 | tf_op jit(solution)/shard_map/reduce_scatter | solution.py:242
  137.7 59.5 %copy-start.8 = (bf16[4,256,256]{1,2,0:T(8,128)(2,1)}, bf16[4,256,256]{1,2,0:T(8,128)(2,1)S(1)}, u32[]{:S(2)}) copy-start(bf16[4,256,256]{1,2,0:T(8,128)(2,1)S(1)} %all-to-all-done.1) | copy-start | bytes 1572868
  187.8 45.7 %copy-start.13 = (bf16[1,256,1024]{2,1,0:T(8,128)(2,1)S(1)}, bf16[1,256,1024]{2,1,0:T(8,128)(2,1)}, u32[]{:S(2)}) copy-start(bf16[1,256,1024]{2,1,0:T(8,128)(2,1)} %param.22) | copy-start | bytes 1572868
  242.3 7.3 %copy-start.17 = (bf16[256,2816]{1,0:T(8,128)(2,1)}, bf16[256,2816]{1,0:T(8,128)(2,1)S(1)}, u32[]{:S(2)}) copy-start(bf16[256,2816]{1,0:T(8,128)(2,1)S(1)} %get-tuple-element.90) | copy-start | bytes 4325380
  242.3 7.3 %copy-start.18 = (bf16[256,2816]{1,0:T(8,128)(2,1)}, bf16[256,2816]{1,0:T(8,128)(2,1)S(1)}, u32[]{:S(2)}) copy-start(bf16[256,2816]{1,0:T(8,128)(2,1)S(1)} %get-tuple-element.91) | copy-start | bytes 4325380
  242.3 7.3 %copy-start.14 = (bf16[1,256,1024]{2,1,0:T(8,128)(2,1)S(1)}, bf16[1,256,1024]{2,1,0:T(8,128)(2,1)}, u32[]{:S(2)}) copy-start(bf16[1,256,1024]{2,1,0:T(8,128)(2,1)} %param.22) | copy-start | bytes 1572868
  252.7 104.3 %reduce-scatter.14.cloned.1.call-start = ((), (), s32[]{:S(2)}) async-start(), calls=%async_computation.18 | async-start | bytes 6488064 | tf_op jit(solution)/shard_map/reduce_scatter | solution.py:242
  258.6 188.8 %reduce-scatter.12.cloned.1.call-start = ((), (), s32[]{:S(2)}) async-start(), calls=%async_computation.17 | async-start | bytes 12976128 | tf_op jit(solution)/shard_map/reduce_scatter | solution.py:242
  266.8 223.0 %reduce-scatter.8.cloned.1.call-start = ((), (), s32[]{:S(2)}) async-start(), calls=%async_computation.15 | async-start | bytes 1769472 | tf_op jit(solution)/shard_map/reduce_scatter | solution.py:242
  305.1 2.9 copy-start.21
  305.2 6.0 slice-start
  308.1 2.7 copy-start.27
  308.1 3.1 slice-start.1
  310.8 1.1 copy-start.10
  311.9 3.5 copy-start.25
  311.9 3.5 copy-start.26
  311.9 4.2 copy-start.33
  319.2 223.3 %reduce-scatter.6.cloned.1.call-start = ((), (), s32[]{:S(2)}) async-start(), calls=%async_computation.14 | async-start | bytes 2621440 | tf_op jit(solution)/shard_map/reduce_scatter | solution.py:234
  328.8 130.2 %all-to-all-start.3 = ((bf16[4,256,256]{1,2,0:T(8,128)(2,1)}), bf16[4,256,256]{1,2,0:T(8,128)(2,1)}, u32[]{:S(2)}, u32[]{:S(2)}) async-start(bf16[4,256,256]{1,2,0:T(8,128)(2,1)} %copy.99), calls=%async_computation.4 | async-start | bytes 1048576 | tf_op jit(solution)/shard_map/all_to_all | solution.py:93
  332.9 310.9 %all-reduce.3.cloned.1.call-start = ((), (), s32[]{:S(2)}) async-start(), calls=%async_computation.19 | async-start | bytes 4849664 | tf_op jit(solution)/shard_map/psum | solution.py:250
  519.9 1.9 copy-start.2
  519.9 2.4 copy-start.5
  546.2 100.4 %copy-start.4 = (f32[128,5632]{1,0:T(8,128)S(1)}, f32[128,5632]{1,0:T(8,128)}, u32[]{:S(2)}) copy-start(f32[128,5632]{1,0:T(8,128)} %param.27) | copy-start | bytes 8650756
  646.6 6.7 %copy-start.7 = (f32[352,1024]{1,0:T(8,128)S(1)}, f32[352,1024]{1,0:T(8,128)}, u32[]{:S(2)}) copy-start(f32[352,1024]{1,0:T(8,128)} %param.28) | copy-start | bytes 4325380
  646.6 6.7 %copy-start.15 = (f32[352,1024]{1,0:T(8,128)S(1)}, f32[352,1024]{1,0:T(8,128)}, u32[]{:S(2)}) copy-start(f32[352,1024]{1,0:T(8,128)} %param.33) | copy-start | bytes 4325380
  646.6 6.7 %copy-start.16 = (f32[352,1024]{1,0:T(8,128)S(1)}, f32[352,1024]{1,0:T(8,128)}, u32[]{:S(2)}) copy-start(f32[352,1024]{1,0:T(8,128)} %param.38) | copy-start | bytes 4325380
  646.6 6.7 %copy-start.22 = (bf16[352,1024]{1,0:T(8,128)(2,1)S(1)}, bf16[352,1024]{1,0:T(8,128)(2,1)}, u32[]{:S(2)}) copy-start(bf16[352,1024]{1,0:T(8,128)(2,1)} %get-tuple-element.74) | copy-start | bytes 2162692
  653.4 2.8 copy-start.30
  653.4 2.8 copy-start.31
  (2 other events, 1.8 us)
Sparse Core Ops, SparseCore 0:
  11.9 28.5 all-gather.9
  42.7 45.9 all-gather.7
  91.2 26.5 all-gather.11
  120.0 67.6 all-gather.13
  190.1 43.3 all-gather.15
  252.9 41.2 reduce-scatter.9
  298.0 59.0 reduce-scatter.13
  360.5 86.7 reduce-scatter.11
  451.2 38.4 reduce-scatter.7
  492.4 50.0 reduce-scatter.5
  545.2 98.5 all-reduce.2

commit v2 on v1

--- a/solution.py
+++ b/solution.py
@@ -1,8 +1,11 @@
+import functools
 import math
 
 import jax
 import jax.numpy as jnp
 from jax import lax
+from jax.experimental import pallas as pl
+from jax.experimental.pallas import tpu as pltpu
 from jax.sharding import PartitionSpec as P
 
 HEAD_DIM = 64
@@ -76,6 +79,628 @@
     second_hat = next_second / (1.0 - BETA_SECOND**STEP)
     new_master = master - rate * (first_hat / (jnp.sqrt(second_hat) + ADAM_EPS) + decay * master)
     return (new_master, next_first, next_second)
+
+
+MESH = pl.DeviceIdType.MESH
+VMEM_BYTES = 58 << 20
+
+
+def full_spec():
+    return pl.BlockSpec(memory_space=pltpu.VMEM)
+
+
+def any_spec():
+    return pl.BlockSpec(memory_space=pl.ANY)
+
+
+class Place:
+    def __init__(self, dp_count, span_count):
+        self.dp_count = dp_count
+        self.span_count = span_count
+        self.inner_count = dp_count // 4
+        self.dp = lax.axis_index("dp")
+        self.span = lax.axis_index("seq")
+        self.core = lax.rem(self.dp, 2)
+        self.inner = lax.rem(self.dp // 2, self.inner_count)
+        self.outer = self.dp // (2 * self.inner_count)
+
+    def at(self, outer, inner, core):
+        return (outer * self.inner_count + inner) * 2 + core
+
+    def inner_plus(self, offset):
+        return lax.rem(self.inner + offset, self.inner_count)
+
+    def greet_all(self):
+        barrier = pltpu.get_barrier_semaphore()
+        for offset in range(1, self.dp_count):
+            pl.semaphore_signal(
+                barrier,
+                inc=1,
+                device_id=(lax.rem(self.dp + offset, self.dp_count), self.span),
+                device_id_type=MESH,
+            )
+        for offset in range(1, self.span_count):
+            pl.semaphore_signal(
+                barrier,
+                inc=1,
+                device_id=(self.dp, lax.rem(self.span + offset, self.span_count)),
+                device_id_type=MESH,
+            )
+        pl.semaphore_wait(barrier, self.dp_count + self.span_count - 2)
+
+
+def remote(source, target, send_sem, recv_sem, device):
+    return pltpu.make_async_remote_copy(
+        src_ref=source,
+        dst_ref=target,
+        send_sem=send_sem,
+        recv_sem=recv_sem,
+        device_id=device,
+        device_id_type=MESH,
+    )
+
+
+def half_rows(rows):
+    return rows // 2 // 16 * 16
+
+
+class Gather:
+    def __init__(self, place, own, whole, send_sems, recv_sems):
+        self.place = place
+        self.own = own
+        self.whole = whole
+        self.rows = own.shape[0]
+        self.send_sems = send_sems
+        self.recv_sems = recv_sems
+        self.sent = []
+        count = place.inner_count
+        self.near, self.lower, self.upper, self.pair = 0, count, 2 * count, 3 * count
+
+    @staticmethod
+    def slots(inner_count):
+        return 6 * inner_count + 1
+
+    def block(self, index, part=None):
+        first = half_rows(self.rows)
+        start, size = {None: (0, self.rows), 0: (0, first), 1: (first, self.rows - first)}[part]
+        return self.whole.at[pl.ds(pl.multiple_of(index * self.rows + start, 16), size), :]
+
+    def send(self, source, target, slot, far_slot, device):
+        copy = remote(
+            source, target, self.send_sems.at[slot], self.recv_sems.at[far_slot], (device, self.place.span)
+        )
+        copy.start()
+        self.sent.append(copy)
+
+    def arrived(self, block, slot):
+        remote(
+            block, block, self.send_sems.at[slot], self.recv_sems.at[slot], (self.place.dp, self.place.span)
+        ).wait_recv()
+
+    def sibling(self, block, slot):
+        place = self.place
+        self.send(block, block, slot, slot, place.at(place.outer, place.inner, 1 - place.core))
+
+    def begin(self):
+        place, count = self.place, self.place.inner_count
+        mine = self.block(place.dp)
+        self.send(self.own, mine, 0, 0, place.at(1 - place.outer, place.inner, place.core))
+        for offset in range(1, count):
+            self.send(
+                self.own,
+                mine,
+                offset,
+                count - offset,
+                place.at(place.outer, place.inner_plus(offset), place.core),
+            )
+        copy = remote(
+            self.own,
+            mine,
+            self.send_sems.at[self.pair],
+            self.recv_sems.at[self.pair],
+            (place.at(place.outer, place.inner, 1 - place.core), place.span),
+        )
+        copy.start()
+        self.sent.append(copy)
+
+    def forward(self):
+        place, count = self.place, self.place.inner_count
+        across = place.at(1 - place.outer, place.inner, place.core)
+        self.arrived(self.block(across), 0)
+        for offset in range(1, count):
+            self.send(
+                self.block(across, 0),
+                self.block(across, 0),
+                self.lower + offset,
+                self.lower + count - offset,
+                place.at(place.outer, place.inner_plus(offset), place.core),
+            )
+        for offset in range(1, count):
+            beside = place.at(place.outer, place.inner_plus(offset), place.core)
+            self.arrived(self.block(beside), offset)
+            self.send(
+                self.block(beside, 1),
+                self.block(beside, 1),
+                self.upper + offset,
+                self.upper + offset,
+                across,
+            )
+        self.sibling(self.block(across), self.pair + count)
+        for offset in range(1, count):
+            beside = place.at(place.outer, place.inner_plus(offset), place.core)
+            self.sibling(self.block(beside), self.pair + offset)
+
+    def share(self):
+        place, count = self.place, self.place.inner_count
+        for offset in range(1, count):
+            far = place.at(1 - place.outer, place.inner_plus(offset), place.core)
+            self.arrived(self.block(far, 0), self.lower + offset)
+            self.sibling(self.block(far, 0), self.pair + count + offset)
+            self.arrived(self.block(far, 1), self.upper + offset)
+            self.sibling(self.block(far, 1), self.pair + 2 * count + offset)
+
+    def end(self):
+        place, count = self.place, self.place.inner_count
+        other = 1 - place.core
+        self.arrived(self.block(place.at(place.outer, place.inner, other)), self.pair)
+        self.arrived(self.block(place.at(1 - place.outer, place.inner, other)), self.pair + count)
+        for offset in range(1, count):
+            inner = place.inner_plus(offset)
+            self.arrived(self.block(place.at(place.outer, inner, other)), self.pair + offset)
+            far = place.at(1 - place.outer, inner, other)
+            self.arrived(self.block(far, 0), self.pair + count + offset)
+            self.arrived(self.block(far, 1), self.pair + 2 * count + offset)
+        for copy in self.sent:
+            copy.wait_send()
+
+
+class Exchange:
+    def __init__(self, place, sources, targets, send_sems, recv_sems):
+        self.place = place
+        self.sources = sources
+        self.targets = targets
+        self.send_sems = send_sems
+        self.recv_sems = recv_sems
+
+    def copy(self, offset):
+        place = self.place
+        count = place.span_count
+        peer = lax.rem(place.span + offset, count)
+        return remote(
+            self.sources.at[peer],
+            self.targets.at[place.span],
+            self.send_sems.at[offset],
+            self.recv_sems.at[count - offset],
+            (place.dp, peer),
+        )
+
+    def start(self):
+        for offset in range(1, self.place.span_count):
+            self.copy(offset).start()
+        self.targets[self.place.span] = self.sources[self.place.span]
+
+    def wait(self):
+        place = self.place
+        count = place.span_count
+        for offset in range(1, count):
+            peer = lax.rem(place.span + offset, count)
+            remote(
+                self.sources.at[peer],
+                self.targets.at[peer],
+                self.send_sems.at[offset],
+                self.recv_sems.at[offset],
+                (place.dp, peer),
+            ).wait_recv()
+
+    def finish(self):
+        for offset in range(1, self.place.span_count):
+            self.copy(offset).wait_send()
+
+
+def cast_rows(source, target):
+    rows = source.shape[0]
+
+    def step(index, unused):
+        at = pl.ds(pl.multiple_of(index * 16, 16), 16)
+        target[at, :] = source[at, :].astype(BF)
+        return unused
+
+    lax.fori_loop(0, rows // 16, step, 0)
+
+
+def swap_halves(rows):
+    width = rows.shape[1]
+    half = HEAD_DIM // 2
+    if width % 128:
+        pieces = []
+        for start in range(0, width, HEAD_DIM):
+            pieces += [rows[:, start + half : start + HEAD_DIM], rows[:, start : start + half]]
+        return jnp.concatenate(pieces, axis=1)
+    lane = lax.broadcasted_iota(jnp.int32, rows.shape, 1)
+    return jnp.where(
+        lane % HEAD_DIM < half, pltpu.roll(rows, width - half, 1), pltpu.roll(rows, half, 1)
+    )
+
+
+def widen(table, width):
+    return jnp.concatenate([table] * (width // table.shape[1]), axis=1)
+
+
+def segment_starts(bounds, rows, first):
+    position = lax.broadcasted_iota(jnp.int32, (rows, 1), 0) + first
+    position = position.astype(F32)
+    start = jnp.zeros((rows, 1), F32)
+    for cut in bounds:
+        start = jnp.where(position >= cut, cut, start)
+    return position, start
+
+
+def head_part(matrix, head):
+    if matrix.shape[1] == HEAD_DIM:
+        return matrix
+    lane = lax.broadcasted_iota(jnp.int32, (1, matrix.shape[1]), 1)
+    return jnp.where(lane // HEAD_DIM == head, matrix, jnp.zeros_like(matrix))
+
+
+def forward_kernel(
+    dp_count,
+    span_count,
+    slot_of,
+    order,
+    tokens,
+    first_values,
+    segments,
+    gains_mine,
+    qkv_mine,
+    out_mine,
+    gate_up_mine,
+    down_mine,
+    cosine,
+    sine,
+    out_whole,
+    gate_up_whole,
+    down_whole,
+    qkv_out,
+    normed_out,
+    gains_out,
+    attended_out,
+    query_out,
+    key_out,
+    value_out,
+    raw_out,
+    lse_out,
+    out_own,
+    gate_up_own,
+    down_own,
+    qkv_whole,
+    gains_all,
+    counts_send,
+    counts_all,
+    first_send,
+    first_all,
+    normed_all,
+    scores_kept,
+    attended_send,
+    attended_all,
+    gather_send,
+    gather_recv,
+    gains_send_sem,
+    gains_recv_sem,
+    counts_send_sem,
+    counts_recv_sem,
+    first_send_sem,
+    first_recv_sem,
+    ring_send,
+    ring_recv,
+    attended_send_sem,
+    attended_recv_sem,
+    local_sem,
+):
+    place = Place(dp_count, span_count)
+    rows, width = tokens.shape
+    group = width // span_count
+    heads = group // HEAD_DIM
+    last = span_count - 1
+    span = place.span
+
+    place.greet_all()
+    gains_all[place.dp] = gains_mine[...]
+    gains_copies = []
+    for offset in range(1, dp_count):
+        peer = lax.rem(place.dp + offset, dp_count)
+        copy = remote(
+            gains_mine,
+            gains_all.at[place.dp],
+            gains_send_sem.at[offset],
+            gains_recv_sem.at[dp_count - offset],
+            (peer, span),
+        )
+        copy.start()
+        gains_copies.append(copy)
+    gathers = [
+        Gather(place, own, whole, gather_send.at[i], gather_recv.at[i])
+        for i, (own, whole) in enumerate(
+            (
+                (qkv_mine, qkv_whole),
+                (out_own, out_whole),
+                (gate_up_own, gate_up_whole),
+                (down_own, down_whole),
+            )
+        )
+    ]
+    qkv_gather, out_gather, gate_up_gather, down_gather = gathers
+    qkv_gather.begin()
+    qkv_whole[pl.ds(pl.multiple_of(place.dp * qkv_mine.shape[0], 16), qkv_mine.shape[0]), :] = (
+        qkv_mine[...]
+    )
+    for index in range(span_count):
+        first_send[index] = first_values[:, index * group : (index + 1) * group]
+    first_exchange = Exchange(place, first_send, first_all, first_send_sem, first_recv_sem)
+    first_exchange.start()
+    ids = segments[...]
+    row = lax.broadcasted_iota(jnp.int32, (8, 128), 0)
+    counts = jnp.zeros((8, 128), F32)
+    for cut in range(3):
+        below = jnp.sum(jnp.where(ids <= cut, 1.0, 0.0), axis=1, keepdims=True)
+        counts = jnp.where(row == cut, below, counts)
+    for index in range(span_count):
+        counts_send[index] = counts
+    counts_exchange = Exchange(place, counts_send, counts_all, counts_send_sem, counts_recv_sem)
+    counts_exchange.start()
+
+    residual = tokens[...].astype(F32)
+    scaled = residual * lax.rsqrt(jnp.mean(residual * residual, axis=1, keepdims=True) + NORM_EPS)
+    for offset in range(1, dp_count):
+        peer = lax.rem(place.dp + offset, dp_count)
+        remote(
+            gains_mine,
+            gains_all.at[peer],
+            gains_send_sem.at[offset],
+            gains_recv_sem.at[offset],
+            (peer, span),
+        ).wait_recv()
+    gains_row = jnp.concatenate([gains_all[i] for i in range(dp_count)], axis=1)
+    gains_out[...] = gains_row
+    normed_all[span] = (scaled * gains_row[0:1, :]).astype(BF)
+
+    def pass_on(block, step, way):
+        return remote(
+            normed_all.at[block],
+            normed_all.at[block],
+            ring_send.at[way, step],
+            ring_recv.at[way, step],
+            (place.dp, jnp.where(way == 0, jnp.minimum(span + 1, last), jnp.maximum(span - 1, 0))),
+        )
+
+    @pl.when(span < last)
+    def up():
+        pass_on(span, 0, 0).start()
+
+    @pl.when(span > 0)
+    def down():
+        pass_on(span, 0, 1).start()
+
+    cast_rows(out_mine, out_own)
+    out_gather.begin()
+    cast_rows(gate_up_mine, gate_up_own)
+    qkv_gather.forward()
+    gate_up_gather.begin()
+    cast_rows(down_mine, down_own)
+    down_gather.begin()
+    own_copies = []
+    for i, member in enumerate(gathers[1:]):
+        copy = pltpu.make_async_copy(member.own, member.block(place.dp), local_sem.at[i])
+        copy.start()
+        own_copies.append(copy)
+    qkv_gather.share()
+    out_gather.forward()
+
+    for step in range(1, span_count):
+
+        @pl.when(span - step >= 0)
+        def from_below():
+            block = jnp.maximum(span - step, 0)
+            pass_on(block, step - 1, 0).wait_recv()
+
+            @pl.when(span < last)
+            def on():
+                pass_on(block, step, 0).start()
+
+        @pl.when(span + step <= last)
+        def from_above():
+            block = jnp.minimum(span + step, last)
+            pass_on(block, step - 1, 1).wait_recv()
+
+            @pl.when(span > 0)
+            def on():
+                pass_on(block, step, 1).start()
+
+    qkv_gather.end()
+    normed_copy = pltpu.make_async_copy(normed_all, normed_out, local_sem.at[3])
+    normed_copy.start()
+    qkv_copy = pltpu.make_async_copy(qkv_whole, qkv_out, local_sem.at[4])
+    qkv_copy.start()
+    first_exchange.wait()
+    counts_exchange.wait()
+    cuts = counts_all[0]
+    for index in range(1, span_count):
+        cuts = cuts + counts_all[index]
+    bounds = [cuts[i : i + 1, 0:1] for i in range(3)]
+
+    def project(position, unused):
+        slot = slot_of[position]
+        mixed = dot_nn(normed_all[slot], qkv_whole[...])
+        cos_here = widen(cosine[position], group)
+        sin_here = widen(sine[position], group)
+        query = mixed[:, :group]
+        key = mixed[:, group : 2 * group]
+        query_out[position] = (query * cos_here + swap_halves(query) * sin_here).astype(BF)
+        key_out[position] = (key * cos_here + swap_halves(key) * sin_here).astype(BF)
+        value_out[position] = (
+            BLEND_MIX * mixed[:, 2 * group :]
+            + (1.0 - BLEND_MIX) * first_all[slot].astype(F32)
+        ).astype(BF)
+        return unused
+
+    lax.fori_loop(0, span_count, project, 0)
+    out_gather.share()
+    gate_up_gather.forward()
+
+    def attend(position, unused):
+        query = query_out[position]
+        parts = [head_part(query, head) for head in range(heads)]
+        query_position, start = segment_starts(bounds, rows, position * rows)
+
+        def score(other, highest):
+            key = key_out[other]
+            key_position = (
+                lax.broadcasted_iota(jnp.int32, (1, rows), 1) + other * rows
+            ).astype(F32)
+            allowed = (key_position <= query_position) & (key_position >= start)
+            found = []
+            for head in range(heads):
+                masked = jnp.where(allowed, dot_nt(parts[head], key) * SCALE, MASK_FILL)
+                scores_kept[head, other] = masked
+                found.append(jnp.maximum(highest[head], jnp.max(masked, axis=1, keepdims=True)))
+            return tuple(found)
+
+        highest = lax.fori_loop(
+            0, position + 1, score, (jnp.full((rows, 1), MASK_FILL, F32),) * heads
+        )
+
+        def raise_scores(other, total):
+            added = []
+            for head in range(heads):
+                raised = jnp.exp(scores_kept[head, other] - highest[head])
+                scores_kept[head, other] = raised
+                added.append(total[head] + jnp.sum(raised, axis=1, keepdims=True))
+            return tuple(added)
+
+        total = lax.fori_loop(
+            0, position + 1, raise_scores, (jnp.zeros((rows, 1), F32),) * heads
+        )
+        inverse = [1.0 / member for member in total]
+
+        def gather_values(other, attended):
+            value = value_out[other]
+            for head in range(heads):
+                weights = (scores_kept[head, other] * inverse[head]).astype(BF)
+                attended = attended + dot_nn(weights, head_part(value, head))
+            return attended
+
+        raw_out[position] = lax.fori_loop(
+            0, position + 1, gather_values, jnp.zeros((rows, group), F32)
+        )
+        lane = lax.broadcasted_iota(jnp.int32, (rows, 128), 1)
+        kept = jnp.zeros((rows, 128), F32)
+        for head in range(heads):
+            kept = jnp.where(lane == head, highest[head] + jnp.log(total[head]), kept)
+        lse_out[position] = kept
+        return unused
+
+    lax.fori_loop(0, span_count // 2, attend, 0)
+    down_gather.forward()
+    lax.fori_loop(span_count // 2, span_count, attend, 0)
+
+    for index in range(span_count):
+        attended_send[index] = raw_out[order[index]].astype(BF)
+    attended_exchange = Exchange(
+        place, attended_send, attended_all, attended_send_sem, attended_recv_sem
+    )
+    attended_exchange.start()
+    gate_up_gather.share()
+    attended_exchange.wait()
+    attended_out[...] = jnp.concatenate([attended_all[i] for i in range(span_count)], axis=1)
+    out_gather.end()
+    down_gather.share()
+    gate_up_gather.end()
+    down_gather.end()
+
+    for copy in gains_copies:
+        copy.wait_send()
+    for exchange in (first_exchange, counts_exchange, attended_exchange):
+        exchange.finish()
+    for step in range(span_count):
+
+        @pl.when((span - step >= 0) & (span < last))
+        def sent_up():
+            pass_on(jnp.maximum(span - step, 0), step, 0).wait_send()
+
+        @pl.when((span + step <= last) & (span > 0))
+        def sent_down():
+            pass_on(jnp.minimum(span + step, last), step, 1).wait_send()
+
+    for copy in own_copies:
+        copy.wait()
+    normed_copy.wait()
+    qkv_copy.wait()
+
+
+def forward_call(
+    dp_count, span_count, slot_of, order, tokens, first_values, segments, gains_mine, qkv_mine,
+    out_mine, gate_up_mine, down_mine, cosine, sine,
+):
+    rows, width = tokens.shape
+    group = width // span_count
+    heads = group // HEAD_DIM
+    owned = qkv_mine.shape[0]
+    doubled = gate_up_mine.shape[1]
+    slots = Gather.slots(dp_count // 4)
+    dma = pltpu.SemaphoreType.DMA
+    by_span = (span_count, rows, group)
+    return pl.pallas_call(
+        functools.partial(forward_kernel, dp_count, span_count),
+        out_shape=(
+            jax.ShapeDtypeStruct((width, width), BF),
+            jax.ShapeDtypeStruct((width, doubled), BF),
+            jax.ShapeDtypeStruct((doubled // 2, width), BF),
+            jax.ShapeDtypeStruct((width, 3 * group), BF),
+            jax.ShapeDtypeStruct((span_count, rows, width), BF),
+            jax.ShapeDtypeStruct((8, width), F32),
+            jax.ShapeDtypeStruct((rows, width), BF),
+            jax.ShapeDtypeStruct(by_span, BF),
+            jax.ShapeDtypeStruct(by_span, BF),
+            jax.ShapeDtypeStruct(by_span, BF),
+            jax.ShapeDtypeStruct(by_span, F32),
+            jax.ShapeDtypeStruct((span_count, rows, 128), F32),
+        ),
+        in_specs=[pl.BlockSpec(memory_space=pltpu.SMEM)] * 2 + [full_spec()] * 10,
+        out_specs=(any_spec(),) * 5 + (full_spec(),) * 7,
+        scratch_shapes=[
+            pltpu.VMEM((owned, width), BF),
+            pltpu.VMEM((owned, doubled), BF),
+            pltpu.VMEM((down_mine.shape[0], width), BF),
+            pltpu.VMEM((width, 3 * group), BF),
+            pltpu.VMEM((dp_count, 8, owned), F32),
+            pltpu.VMEM((span_count, 8, 128), F32),
+            pltpu.VMEM((span_count, 8, 128), F32),
+            pltpu.VMEM(by_span, BF),
+            pltpu.VMEM(by_span, BF),
+            pltpu.VMEM((span_count, rows, width), BF),
+            pltpu.VMEM((heads, span_count, rows, rows), F32),
+            pltpu.VMEM(by_span, BF),
+            pltpu.VMEM(by_span, BF),
+            dma((4, slots)),
+            dma((4, slots)),
+            dma((dp_count,)),
+            dma((dp_count,)),
+            dma((span_count,)),
+            dma((span_count,)),
+            dma((span_count,)),
+            dma((span_count,)),
+            dma((2, span_count)),
+            dma((2, span_count)),
+            dma((span_count,)),
+            dma((span_count,)),
+            dma((5,)),
+        ],
+        compiler_params=pltpu.CompilerParams(
+            collective_id=0, has_side_effects=True, vmem_limit_bytes=VMEM_BYTES
+        ),
+    )(
+        slot_of, order, tokens, first_values, segments, gains_mine, qkv_mine, out_mine,
+        gate_up_mine, down_mine, cosine, sine,
+    )
 
 
 def to_heads(rows, span_count):
@@ -133,55 +758,61 @@
     length = rows_here * span_count
     hidden_width = gate_up_weight.shape[1] // 2
 
-    qkv_owned = qkv_weight.reshape(owned_rows, 3, model_width).astype(BF)
-    qkv_mine = lax.dynamic_slice_in_dim(qkv_owned, mine * group, group, 2).reshape(
-        owned_rows, 3 * group
+    slot_of = jnp.sum(
+        jnp.where(
+            span_order[None, :] == jnp.arange(span_count, dtype=jnp.int32)[:, None],
+            jnp.arange(span_count, dtype=jnp.int32)[None, :],
+            0,
+        ),
+        axis=1,
+    ).astype(jnp.int32)
+    lanes = min(group, 128)
+    lane = jnp.arange(lanes, dtype=jnp.int32) % HEAD_DIM
+    frequency = jnp.exp(
+        (lane % (HEAD_DIM // 2)).astype(F32) * (-math.log(ROPE_BASE) / (HEAD_DIM // 2))
+    )
+    angles = jnp.arange(length, dtype=jnp.int32).astype(F32)[:, None] * frequency[None, :]
+    cosine = jnp.cos(angles).reshape(span_count, rows_here, lanes)
+    sine = (jnp.where(lane < HEAD_DIM // 2, -1.0, 1.0) * jnp.sin(angles)).reshape(
+        span_count, rows_here, lanes
+    )
+    qkv_mine = (
+        lax.dynamic_slice_in_dim(
+            qkv_weight.reshape(owned_rows, 3, model_width), mine * group, group, 2
+        )
+        .reshape(owned_rows, 3 * group)
+        .astype(BF)
     )
     gains_owned = norm_gains.astype(BF).astype(F32)
-    gains_full = lax.all_gather(norm_gains.astype(BF), "dp", axis=0, tiled=True).astype(F32)
-    qkv_copy = lax.all_gather(qkv_mine, "dp", axis=0, tiled=True)
-    out_copy = lax.all_gather(out_weight.astype(BF), "dp", axis=0, tiled=True)
-    gate_up_copy = lax.all_gather(gate_up_weight.astype(BF), "dp", axis=0, tiled=True)
-    down_copy = lax.all_gather(down_weight.astype(BF), "dp", axis=0, tiled=True)
-
-    row_index = jnp.arange(length, dtype=jnp.int32)
-    owner_table = (row_index // rows_here)[:, None] == jnp.arange(span_count, dtype=jnp.int32)[
-        None, :
+    gains_mine = jnp.pad(jnp.transpose(gains_owned), ((0, 6), (0, 0)))
+    (
+        out_copy, gate_up_copy, down_copy, qkv_copy, normed_all, gains_rows, attended,
+        query_pos, key_pos, value_pos, raw_pos, lse_pos,
+    ) = forward_call(
+        lax.axis_size("dp"), span_count, slot_of, span_order, tokens[0], first_values[0], segments,
+        gains_mine, qkv_mine, out_weight, gate_up_weight, down_weight, cosine, sine,
+    )
+    gains_full = jnp.transpose(gains_rows[:2])
+    scaled_in, inverse_in = normalize_parts(residual)
+    normed_all = jnp.take(normed_all, slot_of, axis=0).reshape(length, model_width)
+    all_segments = jnp.take(
+        lax.all_gather(segments[0], "seq", axis=0), slot_of, axis=0
+    ).reshape(length)
+    position = jnp.arange(length)
+    allowed = (all_segments[:, None] == all_segments[None, :]) & (
+        position[None, :] <= position[:, None]
+    )
+    queries, keys, blended, attended_raw = [
+        member.reshape(length, group_heads, HEAD_DIM)
+        for member in (query_pos, key_pos, value_pos, raw_pos)
     ]
-    positions = (
-        jnp.sum(jnp.where(owner_table, span_order[None, :], 0), axis=1) * rows_here
-        + row_index % rows_here
-    )
-    all_segments = lax.all_gather(segments[0], "seq", axis=0, tiled=True)
-    cosine, sine_table = rotary(positions)
-    allowed = (all_segments[:, None] == all_segments[None, :]) & (
-        positions[None, :] <= positions[:, None]
-    )
-
-    scaled_in, inverse_in = normalize_parts(residual)
-    normed_in = (scaled_in * gains_full[:, 0]).astype(BF)
-    normed_all = lax.all_gather(normed_in, "seq", axis=0, tiled=True)
-    first_all = to_heads(first_values[0], span_count)
-    mixed = dot_nn(normed_all, qkv_copy)
-    queries = rotate(
-        mixed[:, :group].reshape(length, group_heads, HEAD_DIM), cosine, sine_table
-    ).astype(BF)
-    keys = rotate(
-        mixed[:, group : 2 * group].reshape(length, group_heads, HEAD_DIM), cosine, sine_table
-    ).astype(BF)
-    blended = (
-        (BLEND_MIX * mixed[:, 2 * group :] + (1.0 - BLEND_MIX) * first_all.astype(F32))
-        .astype(BF)
-        .reshape(length, group_heads, HEAD_DIM)
-    )
+    lse = jnp.transpose(lse_pos.reshape(length, 128)[:, :group_heads])
     scores = jnp.einsum("qhd,khd->hqk", queries, keys, preferred_element_type=F32) * SCALE
-    masked = jnp.where(allowed[None], scores, MASK_FILL)
-    highest = jnp.max(masked, axis=-1, keepdims=True)
-    raised = jnp.where(allowed[None], jnp.exp(masked - highest), 0.0)
-    weights = raised / jnp.sum(raised, axis=-1, keepdims=True)
+    weights = jnp.where(allowed[None], jnp.exp(scores - lse[..., None]), 0.0)
     weights_low = weights.astype(BF)
-    attended_raw = jnp.einsum("hqk,khd->qhd", weights_low, blended, preferred_element_type=F32)
-    attended = to_spans(attended_raw.reshape(length, group).astype(BF), span_count)
+    cos64 = cosine.reshape(length, lanes)[:, None, :32]
+    sin64 = sine.reshape(length, lanes)[:, None, 32:64]
+    cosine, sine_table = cos64, sin64
 
     hidden_mid = residual + dot_nn(attended, out_copy)
     scaled_mid, inverse_mid = normalize_parts(hidden_mid)
@@ -209,6 +840,20 @@
     mid_grad_low = hidden_mid_grad.astype(BF)
     attended_grad = to_heads(dot_nt(mid_grad_low, out_copy).astype(BF), span_count)
 
+    def to_positions(matrix):
+        shape = matrix.shape
+        return jnp.take(
+            matrix.reshape(span_count, rows_here, shape[1]), slot_of, axis=0
+        ).reshape(shape)
+
+    def to_slots(matrix):
+        shape = matrix.shape
+        return jnp.take(
+            matrix.reshape(span_count, rows_here, shape[1]), span_order, axis=0
+        ).reshape(shape)
+
+    attended_grad = to_positions(attended_grad)
+
     heads_grad = attended_grad.reshape(length, group_heads, HEAD_DIM)
     delta = jnp.transpose(jnp.sum(heads_grad.astype(F32) * attended_raw, axis=-1))
     weights_grad = jnp.einsum("qhd,khd->hqk", heads_grad, blended, preferred_element_type=F32)
@@ -222,7 +867,7 @@
     blended_grad = jnp.einsum(
         "hqk,qhd->khd", weights_low, heads_grad, preferred_element_type=F32
     ).astype(BF).reshape(length, group)
-    values_grad = (1.0 - BLEND_MIX) * to_spans(blended_grad, span_count).astype(F32)
+    values_grad = (1.0 - BLEND_MIX) * to_spans(to_slots(blended_grad), span_count).astype(F32)
     mixed_grad = jnp.concatenate(
         [
             rotate(queries_grad, cosine, -sine_table).reshape(length, group),
@@ -232,7 +877,7 @@
         axis=1,
     ).astype(BF)
     normed_in_grad = lax.psum_scatter(
-        dot_nt(mixed_grad, qkv_copy).astype(BF), "seq", scatter_dimension=0, tiled=True
+        to_slots(dot_nt(mixed_grad, qkv_copy).astype(BF)), "seq", scatter_dimension=0, tiled=True
     ).astype(F32)
     tokens_grad = hidden_mid_grad + norm_backward(
         normed_in_grad, scaled_in, inverse_in, gains_full[:, 0]

time: 674 us -> 562 us (0.83)
  waiting for transfers between devices: 380 us -> 186 us
  Pallas kernels: 0 us -> 102 us
  blocking collectives: 70.9 us -> 42.1 us
  local copies, waits for them, and re-layouts: 42.2 us -> 68.8 us
  matrix products: 97.7 us -> 87.2 us
    all_gather x5 -> x0, waiting for transfers between devices: 119 us -> none  [the longest x1 47.4 us: on_device(): lax.all_gather(gate_up_weight.astype(BF), 'dp', axis=0, tiled=True)]
    pallas_call x0 -> x1, Pallas kernels: none -> 102 us  [forward_call(): pl.pallas_call(functools.partial(forward_kernel, dp_count, span_count), o...]
    reduce_scatter x4, waiting for transfers between devices: 143 us -> 80.5 us  [to_owner(): lax.psum_scatter(terms.astype(BF), 'dp', scatter_dimension=0, tiled=True)]
    all_to_all x1 -> x0, blocking collectives: 19.7 us -> none  [to_heads(): lax.all_to_all(rows.reshape(rows.shape[0], span_count, rows.shape[1] // s...]
    all_to_all x2 -> x1, waiting for transfers between devices: 14.5 us -> 0.01 us  [to_spans(): lax.all_to_all(columns.reshape(span_count, rows_here, columns.shape[1]),...]
    convert_element_type x9 -> x2, other arithmetic: 14.3 us -> 0.01 us  [on_device(): jnp.arange(length, dtype=jnp.int32).astype(F32)[:, None]]
    sub x1 -> x0, matrix products: 12.3 us -> none  [on_device(): raised = jnp.where(allowed[None], jnp.exp(masked - highest), 0.0)]
    gather x0 -> x5, local copies, waits for them, and re-layouts: none -> 12.1 us  [the longest x2 5.45 us: to_slots(): jnp.take(matrix.reshape(span_count, rows_here, shape[1]), span_order, axi...]
  transfers between devices with their start and end apart: 14 -> 8, of which waited for: 9 -> 4; matrix products, arithmetic and copies ran while one was open for 22% -> 27% of each run, Pallas kernels for 0% -> 0%
where the time goes in v2:
time: 562 us; the launch traced here: 552 us
  waiting for transfers between devices  186 us (33%)
  Pallas kernels  102 us (18%)
  matrix products  87.2 us (16%)
  local copies, waits for them, and re-layouts  68.8 us (12%)
  blocking collectives  42.1 us (7%)
  other arithmetic  41.6 us (7%)
  between operations  14.9 us (3%)
  starting transfers between devices  9.43 us (2%)
    pallas_call x1, Pallas kernels, forward_call(): pl.pallas_call(functools.partial(forward_kernel, dp_count, span_count), o...  102 us
    psum x1, waiting for transfers between devices, on_device(): lax.psum((to_owner(dot_tn(attended, mid_grad_low)), to_owner(dot_tn(norme...  97.1 us
    reduce_scatter x4, waiting for transfers between devices, to_owner(): lax.psum_scatter(terms.astype(BF), 'dp', scatter_dimension=0, tiled=True)  80.5 us
    all_gather x1, blocking collectives, on_device(): lax.all_gather(to_owner(dot_tn(normed_all, mixed_grad)), 'seq', axis=0)  26.8 us
    unnamed x79, local copies, waits for them, and re-layouts  21.7 us
    dot_general x4, matrix products, dot_nt(): lax.dot_general(left, right, (((1,), (1,)), ((), ())), preferred_element_...  19.3 us
    dot_general x4, matrix products, dot_tn(): lax.dot_general(left, right, (((0,), (0,)), ((), ())), preferred_element_...  18.8 us
    sub x5, other arithmetic, apply_adamw(): master - rate * (first_hat / (jnp.sqrt(second_hat) + ADAM_EPS) + decay *...  17.4 us
  transfers between devices with their start and end apart: 8, of which 4 were waited for; matrix products, arithmetic and copies ran while one was open for 27% of the time, Pallas kernels for 0%

profile of v2, /device:TPU:0, one launch (start us, length us, event | category | flops | bytes accessed | tf_op | source)
XLA Modules:
  0.0 552.3 jit_solution(15829356480316756615)
XLA Ops:
  12.8 3.0 fusion.36
  15.8 102.2 %shard_map.331 = (bf16[1024,1024]{1,0:T(8,128)(2,1)}, bf16[1024,5632]{1,0:T(8,128)(2,1)}, bf16[2816,1024]{1,0:T(8,128)(2,1)}, bf16[1024,768]{1,0:T(8,128)(2,1)},...) custom-call(s32[4]{0:T(128)} %select_reduce_fusion.slot_of, ...), custom_call_target="tpu_custom_call" | custom-call | tf_op jit(solution)/shard_map/pallas_call | solution.py:651
  118.8 2.7 multiply_reduce_fusion.2
  121.6 6.3 %fusion.56 = f32[256,5632]{1,0:T(8,128)S(1)} fusion(bf16[1024,5632]{1,0:T(8,128)(2,1)} %get-tuple-element.35, f32[256,1024]{1,0:T(8,128)S(1)} %get-tuple-element.134, f32[1024]{0:T(1024)S(1)} %bitcast.131, f32[256]{0:T(256)S(1)} %add_rsqrt_fusion.1), kind=kOutput, calls=%fused_computation.147 | convolution fusion | flops 2953576448 | bytes 18355200 | tf_op jit(solution)/shard_map/dot_general | solution.py:32
  127.9 3.9 multiply_convert_fusion.2
  131.8 7.2 %multiply_reduce_fusion.1 = (f32[256]{0:T(256)S(1)}, f32[256,1024]{1,0:T(8,128)S(1)}) fusion(f32[256,1024]{1,0:T(8,128)S(1)} %get-tuple-element.134, f32[256]{0:T(256)S(1)} %add_rsqrt_fusion.1, f32[1024]{0:T(1024)S(1)} %bitcast.132, bf16[1024,5632]{1,0:T(8,128)(2,1)} %get-tuple-element.35, bf16[256,2816]{1,0:T(8,128)(2,1)S(1)} %get-tuple-element.117, ...), kind=kOutput, calls=%fused_computation.76 | convolution fusion | flops 2959605504 | bytes 16521216 | tf_op jit(solution)/shard_map/dot_general | solution.py:36
  140.1 2.1 convolution_convert_fusion.2
  142.4 5.6 %convolution_convert_fusion.1 = bf16[2816,1024]{1,0:T(8,128)(2,1)} fusion(bf16[256,2816]{1,0:T(8,128)(2,1)} %get-tuple-element.118, bf16[1,256,1024]{2,1,0:T(8,128)(2,1)S(1)} %copy-done.11), kind=kOutput, calls=%fused_computation.11 | convolution fusion | flops 1479278592 | bytes 7733248 | tf_op jit(solution)/shard_map/dot_general | solution.py:40
  148.1 8.2 %convolution_convert_fusion = bf16[1024,5632]{1,0:T(8,128)(2,1)} fusion(bf16[256,2816]{1,0:T(8,128)(2,1)} %copy-done.15, bf16[256,2816]{1,0:T(8,128)(2,1)} %copy-done.14, f32[256,1024]{1,0:T(8,128)S(1)} %get-tuple-element.134, f32[1024]{0:T(1024)S(1)} %bitcast.133, f32[256]{0:T(256)S(1)} %add_rsqrt_fusion.1), kind=kOutput, calls=%fused_computation.8 | convolution fusion | flops 2965110784 | bytes 15471616 | tf_op jit(solution)/shard_map/dot_general | solution.py:40
  156.3 2.3 convolution_convert_fusion.5
  159.5 4.1 all-to-all-start
  163.7 15.2 %all-gather.1 = s32[4,1,256]{2,1,0:T(1,128)S(1)} all-gather(s32[1,1,256]{2,1,0:T(1,128)S(1)} %bitcast.138), channel_id=1, replica_groups=mesh['dp'=8,'seq'=4] {'seq'}, dimensions={0}, use_global_device_ids=true | all-gather | bytes 5120 | tf_op jit(solution)/shard_map/all_gather | solution.py:799
  179.7 3.7 gather_fusion.4
  184.3 3.2 broadcast_select_fusion
  192.4 2.1 copy.112
  194.5 2.3 reshape.289
  198.1 2.2 copy.117
  200.3 2.2 reshape.293
  202.5 2.5 copy.118
  205.1 2.7 reshape.294
  207.8 9.2 %fusion.64 = f32[4,1024,1024]{2,1,0:T(8,128)} fusion(bf16[1024,4,64]{0,2,1:T(8,128)(2,1)S(1)} %reshape.290, bf16[1024,4,64]{0,2,1:T(8,128)(2,1)} %reshape.289), kind=kOutput, calls=%fused_computation.149 | convolution fusion | flops 536870912 | bytes 17825792 | tf_op jit(solution)/shard_map/qhd,khd->hqk/dot_general | solution.py:810
  217.0 2.4 gather_fusion.1
  221.4 2.1 copy.116
  223.5 2.2 reshape_reshape.10
  227.2 12.6 %multiply_convert_fusion = bf16[4,1024,1024]{2,1,0:T(8,128)(2,1)} fusion(f32[4,1024,1024]{2,1,0:T(8,128)} %fusion.64, bf16[1024,4,64]{0,2,1:T(8,128)(2,1)} %reshape_reshape.10, bf16[1024,4,64]{0,2,1:T(8,128)(2,1)} %reshape.293, f32[4,1024]{1,0:T(4,128)S(1)} %bitcast.137, f32[4,1024]{1,0:T(4,128)S(1)} %copy.114, pred[1024,1024]{1,0:T(8,128)(4,1)} %fusion.4), kind=kOutput, calls=%fused_computation.5 | convolution fusion | flops 562036736 | bytes 27295744 | tf_op jit(solution)/shard_map/qhd,khd->hqk/dot_general | solution.py:859
  239.8 7.4 %fusion.20 = f32[1024,4,64]{0,2,1:T(8,128)} fusion(bf16[1024,4,64]{0,2,1:T(8,128)(2,1)} %reshape.289, bf16[4,1024,1024]{2,1,0:T(8,128)(2,1)} %multiply_convert_fusion), kind=kOutput, calls=%fused_computation.57 | convolution fusion | flops 537657344 | bytes 9961472 | tf_op jit(solution)/shard_map/hqk,khd->qhd/dot_general | solution.py:862
  250.5 3.8 multiply_convert_fusion.4
  255.1 3.0 convolution_convert_fusion.4
  258.4 5.8 %convolution_convert_fusion.3 = bf16[1024,1024]{1,0:T(8,128)(2,1)} fusion(bf16[1024,768]{1,0:T(8,128)(2,1)} %get-tuple-element.42, bf16[1024,256]{0,1:T(8,128)(2,1)} %bitcast.144, bf16[1024,256]{0,1:T(8,128)(2,1)} %bitcast.127, bf16[1024,256]{0,1:T(8,128)(2,1)} %bitcast.129), kind=kOutput, calls=%fused_computation.35 | convolution fusion | flops 1616379904 | bytes 5242880 | tf_op jit(solution)/shard_map/dot_general | solution.py:36
  264.2 4.1 gather_fusion.2
  268.3 3.3 broadcast_select_fusion.1
  277.6 4.7 all-to-all-start.1
  282.4 53.8 %reduce-scatter.12.cloned.1.call-done = bf16[128,5632]{1,0:T(8,128)(2,1)} async-done(((bf16[1024,5632]{1,0:T(8,128)(2,1)}), bf16[128,5632]{1,0:T(8,128)(2,1)}) %reduce-scatter.12.cloned.1.call-update) | async-done | bytes 1441808 | tf_op jit(solution)/shard_map/reduce_scatter | solution.py:887
  336.2 3.0 copy.121
  339.2 3.0 copy.124
  342.3 5.5 %fusion.29 = bf16[1,256,1024]{2,1,0:T(8,128)(2,1)} fusion(f32[256,1024]{1,0:T(8,128)S(1)} %get-tuple-element.134, bf16[256,2816]{1,0:T(8,128)(2,1)} %get-tuple-element.118, bf16[2816,1024]{1,0:T(8,128)(2,1)} %get-tuple-element.36), kind=kOutput, calls=%fused_computation.64 | convolution fusion | flops 1476919296 | bytes 8781824 | tf_op jit(solution)/shard_map/dot_general | solution.py:32
  349.2 2.6 copy.128
  351.8 26.6 %reduce-scatter.8.cloned.1.call-done = bf16[128,768]{1,0:T(8,128)(2,1)} async-done(((bf16[1024,768]{1,0:T(8,128)(2,1)}), bf16[128,768]{1,0:T(8,128)(2,1)}) %reduce-scatter.8.cloned.1.call-update) | async-done | bytes 196624 | tf_op jit(solution)/shard_map/reduce_scatter | solution.py:887
  378.4 26.8 %all-gather = bf16[512,768]{1,0:T(8,128)(2,1)} all-gather(bf16[128,768]{1,0:T(8,128)(2,1)} %reduce-scatter.8.cloned.1.call-done), channel_id=2, replica_groups=mesh['dp'=8,'seq'=4] {'seq'}, dimensions={0}, use_global_device_ids=true | all-gather | bytes 983040 | tf_op jit(solution)/shard_map/all_gather | solution.py:889
  410.7 4.5 multiply_subtract_fusion.1
  415.2 3.1 copy.129
  418.3 3.0 copy.130
  422.9 8.6 %reduce-scatter.6.cloned.1.call-done = bf16[256,1024]{1,0:T(8,128)(2,1)} async-done(((bf16[1024,1024]{1,0:T(8,128)(2,1)}), bf16[256,1024]{1,0:T(8,128)(2,1)}) %reduce-scatter.6.cloned.1.call-update) | async-done | bytes 524304 | tf_op jit(solution)/shard_map/reduce_scatter | solution.py:879
  432.9 2.3 fusion.34
  435.2 97.1 %all-reduce.4.cloned.1.call-done = (bf16[128,1024]{1,0:T(8,128)(2,1)}, bf16[128,5632]{1,0:T(8,128)(2,1)}, bf16[352,1024]{1,0:T(8,128)(2,1)}) async-done(((bf16[128,1024]{1,0:T(8,128)(2,1)}, bf16[128,5632]{1,0:T(8,128)(2,1)}, bf16[352,1024]{1,0:T(8,128)(2,1)}), (bf16[128,1024]{1,0:T(8,128)(2,1)}, bf16[128,5632]{1,0:T(8,128)(2,1)}, bf16[352,1024]{1,0:T(8,128)(2,1)})) %all-reduce.4.cloned.1.call-update) | async-done | bytes 2424848 | tf_op jit(solution)/shard_map/psum | solution.py:895
  532.3 2.8 multiply_subtract_fusion.3
  535.1 6.7 %multiply_subtract_fusion = (f32[128,5632]{1,0:T(8,128)}, f32[128,5632]{1,0:T(8,128)}, f32[128,5632]{1,0:T(8,128)}, f32[128]{0:T(128)S(1)}) fusion(f32[128,5632]{1,0:T(8,128)S(1)} %copy-done.2, bf16[128,5632]{1,0:T(8,128)(2,1)} %get-tuple-element.99, f32[128,5632]{1,0:T(8,128)} %param.36, f32[128,5632]{1,0:T(8,128)} %param.41), kind=kLoop, calls=%fused_computation.22 | loop fusion | flops 13696896 | bytes 18743808 | tf_op jit(solution)/shard_map/sub | solution.py:80
  541.9 2.8 multiply_subtract_fusion.2
  (144 shorter events, 40.8 us)
Async XLA Ops:
  7.2 275.2 %reduce-scatter.10.cloned.1.call-start = ((), (), s32[]{:S(2)}) async-start(), calls=%async_computation.9 | async-start | bytes 2359296 | tf_op jit(solution)/shard_map/reduce_scatter | solution.py:887
  11.1 106.9 %copy-start.3 = (f32[128,3072]{0,1:T(8,128)}, f32[128,3072]{0,1:T(8,128)S(1)}, u32[]{:S(2)}) copy-start(f32[128,3072]{0,1:T(8,128)S(1)} %copy.109) | copy-start | bytes 4718596
  15.8 103.0 %copy-start.1 = (bf16[1,256,1024]{2,1,0:T(8,128)(2,1)S(1)}, bf16[1,256,1024]{2,1,0:T(8,128)(2,1)}, u32[]{:S(2)}) copy-start(bf16[1,256,1024]{2,1,0:T(8,128)(2,1)} %param.24) | copy-start | bytes 1572868
  118.8 9.0 %slice-start.4 = ((s8[5767168]{0:T(1024)(128)(4,1)}), s8[4194304]{0:T(1024)(128)(4,1)S(1)}, s32[]{:S(2)}) async-start(s8[5767168]{0:T(1024)(128)(4,1)} %bitcast.141), calls=%async_computation.17 | async-start | bytes 8388608
  121.5 6.3 %copy-start.11 = (bf16[1,256,1024]{2,1,0:T(8,128)(2,1)S(1)}, bf16[1,256,1024]{2,1,0:T(8,128)(2,1)}, u32[]{:S(2)}) copy-start(bf16[1,256,1024]{2,1,0:T(8,128)(2,1)} %param.26) | copy-start | bytes 1572868
  121.5 6.3 %slice-start.5 = ((s8[5767168]{0:T(1024)(128)(4,1)}), s8[1572864]{0:T(1024)(128)(4,1)S(1)}, s32[]{:S(2)}) async-start(s8[5767168]{0:T(1024)(128)(4,1)} %bitcast.141), calls=%async_computation.18 | async-start | bytes 3145728
  131.8 7.2 %copy-start.14 = (bf16[256,2816]{1,0:T(8,128)(2,1)}, bf16[256,2816]{1,0:T(8,128)(2,1)S(1)}, u32[]{:S(2)}) copy-start(bf16[256,2816]{1,0:T(8,128)(2,1)S(1)} %get-tuple-element.116) | copy-start | bytes 4325380
  131.8 7.2 %copy-start.15 = (bf16[256,2816]{1,0:T(8,128)(2,1)}, bf16[256,2816]{1,0:T(8,128)(2,1)S(1)}, u32[]{:S(2)}) copy-start(bf16[256,2816]{1,0:T(8,128)(2,1)S(1)} %get-tuple-element.117) | copy-start | bytes 4325380
  139.0 1.0 copy-start.8
  142.2 140.2 %reduce-scatter.14.cloned.1.call-start = ((), (), s32[]{:S(2)}) async-start(), calls=%async_computation.11 | async-start | bytes 6488064 | tf_op jit(solution)/shard_map/reduce_scatter | solution.py:887
  148.0 188.2 %reduce-scatter.12.cloned.1.call-start = ((), (), s32[]{:S(2)}) async-start(), calls=%async_computation.10 | async-start | bytes 12976128 | tf_op jit(solution)/shard_map/reduce_scatter | solution.py:887
  156.3 7.5 %copy-start.22 = (s32[1,256]{1,0:T(1,128)S(1)}, s32[1,256]{1,0:T(1,128)}, u32[]{:S(2)}) copy-start(s32[1,256]{1,0:T(1,128)} %segments.1) | copy-start | bytes 3076
  156.3 22.7 %copy-start.27 = (s32[4]{0:T(128)S(1)}, s32[4]{0:T(128)}, u32[]{:S(2)}) copy-start(s32[4]{0:T(128)} %select_reduce_fusion.slot_of) | copy-start | bytes 52
  159.5 57.5 %all-to-all-start = ((bf16[256,4,256]{2,0,1:T(8,128)(2,1)}), bf16[256,4,256]{2,0,1:T(8,128)(2,1)}, u32[]{:S(2)}, u32[]{:S(2)}) async-start(bf16[256,4,256]{2,0,1:T(8,128)(2,1)} %bitcast.111), calls=%async_computation | async-start | bytes 1048576 | tf_op jit(solution)/shard_map/all_to_all | solution.py:707
  163.6 214.8 %reduce-scatter.8.cloned.1.call-start = ((), (), s32[]{:S(2)}) async-start(), calls=%async_computation.8 | async-start | bytes 1769472 | tf_op jit(solution)/shard_map/reduce_scatter | solution.py:887
  179.7 3.8 copy-start.19
  184.3 5.6 %copy-start.18 = (bf16[4,256,256]{2,1,0:T(8,128)(2,1)S(1)}, bf16[4,256,256]{2,1,0:T(8,128)(2,1)}, u32[]{:S(2)}) copy-start(bf16[4,256,256]{2,1,0:T(8,128)(2,1)} %get-tuple-element.38) | copy-start | bytes 1572868
  227.2 22.1 %slice-start = ((s8[16777216]{0:T(1024)(128)(4,1)}), s8[4194304]{0:T(1024)(128)(4,1)S(1)}, s32[]{:S(2)}) async-start(s8[16777216]{0:T(1024)(128)(4,1)} %bitcast.113), calls=%async_computation.13 | async-start | bytes 8388608
  227.2 22.1 %slice-start.1 = ((s8[16777216]{0:T(1024)(128)(4,1)}), s8[4194304]{0:T(1024)(128)(4,1)S(1)}, s32[]{:S(2)}) async-start(s8[16777216]{0:T(1024)(128)(4,1)} %bitcast.113), calls=%async_computation.14 | async-start | bytes 8388608
  227.2 22.1 %slice-start.2 = ((s8[16777216]{0:T(1024)(128)(4,1)}), s8[4194304]{0:T(1024)(128)(4,1)S(1)}, s32[]{:S(2)}) async-start(s8[16777216]{0:T(1024)(128)(4,1)} %bitcast.113), calls=%async_computation.15 | async-start | bytes 8388608
  239.8 7.4 %copy-start = (bf16[4,1024,1024]{2,1,0:T(8,128)(2,1)S(1)}, bf16[4,1024,1024]{2,1,0:T(8,128)(2,1)}, u32[]{:S(2)}) copy-start(bf16[4,1024,1024]{2,1,0:T(8,128)(2,1)} %multiply_convert_fusion) | copy-start | bytes 25165828
  247.2 1.6 copy-start.7
  247.2 2.5 slice-start.3
  248.8 1.3 copy-start.9
  248.8 1.7 copy-start.16
  249.2 5.1 copy-start.20
  250.5 3.8 copy-start.21
  250.5 4.6 copy-start.10
  254.3 0.8 copy-start.28
  255.1 3.2 copy-start.26
  258.1 173.4 %reduce-scatter.6.cloned.1.call-start = ((), (), s32[]{:S(2)}) async-start(), calls=%async_computation.7 | async-start | bytes 2621440 | tf_op jit(solution)/shard_map/reduce_scatter | solution.py:879
  277.6 70.2 %all-to-all-start.1 = ((bf16[4,256,256]{2,1,0:T(8,128)(2,1)}), bf16[4,256,256]{2,1,0:T(8,128)(2,1)S(1)}, u32[]{:S(2)}, u32[]{:S(2)}) async-start(bf16[4,256,256]{2,1,0:T(8,128)(2,1)} %broadcast_select_fusion.2), calls=%async_computation.2 | async-start | bytes 1048576 | tf_op jit(solution)/shard_map/all_to_all | solution.py:718
  282.3 249.9 %all-reduce.4.cloned.1.call-start = ((), (), s32[]{:S(2)}) async-start(), calls=%async_computation.12 | async-start | bytes 4849664 | tf_op jit(solution)/shard_map/psum | solution.py:895
  408.3 1.9 copy-start.4
  408.3 2.4 copy-start.5
  435.2 99.9 %copy-start.2 = (f32[128,5632]{1,0:T(8,128)S(1)}, f32[128,5632]{1,0:T(8,128)}, u32[]{:S(2)}) copy-start(f32[128,5632]{1,0:T(8,128)} %gate_up_mine.1) | copy-start | bytes 8650756
  535.1 6.7 %copy-start.6 = (f32[352,1024]{1,0:T(8,128)S(1)}, f32[352,1024]{1,0:T(8,128)}, u32[]{:S(2)}) copy-start(f32[352,1024]{1,0:T(8,128)} %down_mine.1) | copy-start | bytes 4325380
  535.1 6.7 %copy-start.12 = (f32[352,1024]{1,0:T(8,128)S(1)}, f32[352,1024]{1,0:T(8,128)}, u32[]{:S(2)}) copy-start(f32[352,1024]{1,0:T(8,128)} %param.37) | copy-start | bytes 4325380
  535.1 6.7 %copy-start.13 = (f32[352,1024]{1,0:T(8,128)S(1)}, f32[352,1024]{1,0:T(8,128)}, u32[]{:S(2)}) copy-start(f32[352,1024]{1,0:T(8,128)} %param.42) | copy-start | bytes 4325380
  535.1 6.7 %copy-start.17 = (bf16[352,1024]{1,0:T(8,128)(2,1)S(1)}, bf16[352,1024]{1,0:T(8,128)(2,1)}, u32[]{:S(2)}) copy-start(bf16[352,1024]{1,0:T(8,128)(2,1)} %get-tuple-element.100) | copy-start | bytes 2162692
  541.9 2.8 copy-start.23
  541.9 2.8 copy-start.24
  541.9 2.8 copy-start.25
Sparse Core Ops, SparseCore 0:
  142.3 40.5 reduce-scatter.9
  186.8 59.0 reduce-scatter.13
  249.4 86.7 reduce-scatter.11
  339.9 38.4 reduce-scatter.7
  381.1 50.3 reduce-scatter.5
  434.1 98.1 all-reduce.3
